TPU v7x, 512 devices: a whole 4x4x16 slice. The times are simulated.
512 devices in a mesh: grp: 16 (over x, y), sub: 32 (over z, core).
Axes of the slice: x: 4, y: 4, z: 16, core: 2. Of those that a mesh axis runs over, the one named last changes fastest.
Arguments:
- vectors: float32 [16, 256, 640, 128], P(None, 'grp', 'sub'), may hold values from -0.03125 to 0.03125
- permeability: float32 [256, 512, 128], P('grp', 'sub'), may hold values from 0.05 to 20
- counts: int32 [16, 32], P('grp', 'sub'), may hold values from 4 to 16
- ownership: int32 [16, 32], P('grp'), may hold values from 0 to 31, each once within a row
Outputs:
- coarse_rows: float32 [16, 32, 16, 144], P('grp')
Inputs may be any that keep to these rules, and one draw needn't show every extreme that they name: Each subdomain keeps its first counts vectors. `ownership`: each group's row names every subdomain index of that group once.
All inputs are finite; a program needn't handle non-finite values.
Results may differ from a plain program's by a relative error of at most 0.0003.
Values sent between devices are 32-bit elements; how exact they have to be, the bound alone decides.
A program may use at most 128 MiB of HBM per device.

v0:
```python
import jax
import jax.numpy as jnp
from jax import lax
from jax.sharding import PartitionSpec as P


def extended_2(cells, sides, width):
    for axis, dim in sides:
        count = lax.axis_size(axis)
        ends = count - 1
        head = lax.slice_in_dim(cells, 0, width, axis=dim)
        tail = lax.slice_in_dim(cells, cells.shape[dim] - width, cells.shape[dim], axis=dim)
        cells = jnp.concatenate(
            [
                lax.ppermute(tail, axis, [(i, (i + 1) % count) for i in range(ends)]),
                cells,
                lax.ppermute(head, axis, [((i + 1) % count, i) for i in range(ends)]),
            ],
            axis=dim,
        )
    return cells


def harmonic(first_perm, second_perm):
    return 2.0 * first_perm * second_perm / (first_perm + second_perm)


def stack_vectors(extended, margin, depth):
    reach = margin + 1
    height = depth + 2
    below = extended[:, :, :reach]
    middle = extended[:, :, 2 * margin : 2 * margin + height]
    above = extended[:, :, extended.shape[2] - reach :]
    filler = jnp.zeros(
        (below.shape[0], below.shape[1], height - reach, below.shape[3]), extended.dtype
    )
    below_full = jnp.concatenate([below, filler], axis=2)
    above_full = jnp.concatenate([filler, above], axis=2)
    return jnp.concatenate([below_full, middle, above_full], axis=0)


def per_device(vectors, permeability, counts, ownership):
    highest = lax.Precision.HIGHEST
    vec_total = vectors.shape[0]
    depth = permeability.shape[1]
    extent = vectors.shape[2]
    margin = (extent - depth) // 2
    n_sub = lax.axis_size("sub")
    n_grp = lax.axis_size("grp")
    sub_index = lax.axis_index("sub")
    grp_index = lax.axis_index("grp")
    levels = sub_index * depth - margin + jnp.arange(extent, dtype=jnp.int32)
    level_keep = ((levels >= 0) & (levels < n_sub * depth)).astype(jnp.float32)
    vector_keep = (jnp.arange(vec_total, dtype=jnp.int32) < counts[0, 0]).astype(jnp.float32)
    masked = vectors * level_keep[None, None, :, None] * vector_keep[:, None, None, None]
    extended = extended_2(masked, (("sub", 2),), margin + 1)
    stacked = stack_vectors(extended, margin, depth)
    inner = stacked[:, :, 1:-1]
    sides = extended_2(inner, (("grp", 1),), 1)
    left_face = sides[:, 0]
    right_face = sides[:, -1]
    rims = extended_2(permeability, (("grp", 0), ("sub", 1)), 1)
    first_x = jnp.where(grp_index == 0, permeability[0], rims[0, 1:-1])
    last_x = jnp.where(grp_index == n_grp - 1, permeability[-1], rims[-1, 1:-1])
    first_z = jnp.where(sub_index == 0, permeability[:, 0], rims[1:-1, 0])
    last_z = jnp.where(sub_index == n_sub - 1, permeability[:, -1], rims[1:-1, -1])
    coef_xup = harmonic(permeability, jnp.concatenate([permeability[1:], last_x[None]], axis=0))
    coef_xdown = harmonic(permeability, jnp.concatenate([first_x[None], permeability[:-1]], axis=0))
    coef_zup = harmonic(
        permeability, jnp.concatenate([permeability[:, 1:], last_z[:, None]], axis=1)
    )
    coef_zdown = harmonic(
        permeability, jnp.concatenate([first_z[:, None], permeability[:, :-1]], axis=1)
    )
    coef_yup = harmonic(
        permeability, jnp.concatenate([permeability[:, :, 1:], permeability[:, :, -1:]], axis=2)
    )
    coef_ydown = harmonic(
        permeability, jnp.concatenate([permeability[:, :, :1], permeability[:, :, :-1]], axis=2)
    )
    centre = stacked[:, :, 1:-1]
    zero_plane = jnp.zeros((centre.shape[0], 1, centre.shape[2], centre.shape[3]), jnp.float32)
    zero_line = jnp.zeros((centre.shape[0], centre.shape[1], centre.shape[2], 1), jnp.float32)
    applied = coef_xup * (centre - jnp.concatenate([centre[:, 1:], zero_plane], axis=1))
    applied = applied + coef_xdown * (
        centre - jnp.concatenate([zero_plane, centre[:, :-1]], axis=1)
    )
    applied = applied + coef_zup * (centre - stacked[:, :, 2:])
    applied = applied + coef_zdown * (centre - stacked[:, :, :-2])
    applied = applied + coef_yup * (centre - jnp.concatenate([centre[..., 1:], zero_line], axis=3))
    applied = applied + coef_ydown * (
        centre - jnp.concatenate([zero_line, centre[..., :-1]], axis=3)
    )
    self_gram = jnp.einsum("axzy,bxzy->ab", centre, applied, precision=highest)
    right_gram = -jnp.einsum(
        "azy,bzy->ab", centre[:, -1] * coef_xup[-1], right_face, precision=highest
    )
    left_gram = -jnp.einsum(
        "azy,bzy->ab", centre[:, 0] * coef_xdown[0], left_face, precision=highest
    )
    grams = [
        matrix.reshape(3, vec_total, 3, vec_total) for matrix in (left_gram, self_gram, right_gram)
    ]
    zero_block = jnp.zeros((vec_total, vec_total), jnp.float32)
    row_parts = []
    for row_slot in range(3):
        pieces = []
        for matrix in grams:
            for offset in (-1, 0, 1):
                col_slot = row_slot + offset
                pieces.append(matrix[row_slot, :, col_slot, :] if 0 <= col_slot < 3 else zero_block)
        row_parts.append(jnp.concatenate(pieces, axis=1))
    partial_rows = jnp.stack(row_parts, axis=0)
    targets = sub_index + jnp.arange(3, dtype=jnp.int32) - 1
    selector = (ownership[0][:, None] == targets[None, :]).astype(jnp.float32)
    placed = jnp.einsum("ja,akc->jkc", selector, partial_rows, precision=highest)
    owned = lax.psum_scatter(placed, "sub", scatter_dimension=0, tiled=True)
    gathered = lax.all_gather(owned, "sub", axis=0, tiled=True)
    return gathered[None]


def solution(mesh):
    in_specs = (P(None, "grp", "sub", None), P("grp", "sub", None), P("grp", "sub"), P("grp", None))
    out_specs = P("grp", None, None, None)
    return jax.shard_map(
        per_device, mesh=mesh, in_specs=in_specs, out_specs=out_specs, check_vma=False
    )
```

profile of v0, /device:TPU:1, one launch (start us, length us, event | category | flops | bytes accessed | tf_op | source)
XLA Modules:
  0.0 257.5 jit_solution(11548488872593905208)
XLA Ops:
  6.5 1.4 fusion.60
  7.9 1.3 collective-permute-start.4
  9.2 5.3 %collective-permute-start.2 = (f32[1,16,128]{2,1,0:T(8,128)S(1)}, f32[1,16,128]{2,1,0:T(8,128)}, u32[]{:S(2)}, u32[]{:S(2)}) collective-permute-start(f32[1,16,128]{2,1,0:T(8,128)S(1)} %get-tuple-element.30), channel_id=1, source_target_pairs={{0,32},{32,64},{64,96},{96,128},{128,160},{160,192},{192,224},{224... | collective-permute-start | bytes 24584 | tf_op jit(solution)/shard_map/ppermute | solution.py:15
  15.1 3.3 %fusion.29 = f32[16,16,20,128]{3,0,2,1:T(8,128)S(1)} fusion(f32[16,16,20,128]{3,1,2,0:T(8,128)} %param.4, f32[16]{0:T(128)S(1)} %compare_convert_fusion, f32[20]{0:T(128)S(1)} %and_convert_fusion), kind=kLoop, calls=%fused_computation.34 | loop fusion | flops 1310720 | bytes 5243024 | tf_op jit(solution)/shard_map/mul | solution.py:55
  18.4 1.0 fusion.56
  19.3 4.8 %collective-permute-start = (f32[16,16,3,128]{3,0,2,1:T(8,128)}, f32[16,16,3,128]{3,0,2,1:T(8,128)}, u32[]{:S(2)}, u32[]{:S(2)}) collective-permute-start(f32[16,16,3,128]{3,0,2,1:T(8,128)} %get-tuple-element.11), channel_id=1, source_target_pairs={{0,1},{1,2},{2,3},{3,4},{4,5},{5,6},{6,7},{7,8},{8,9},{9,10},{10,1... | collective-permute-start | bytes 1179656 | tf_op jit(solution)/shard_map/ppermute | solution.py:15
  24.2 5.9 %collective-permute-start.1 = (f32[16,16,3,128]{3,0,2,1:T(8,128)}, f32[16,16,3,128]{3,0,2,1:T(8,128)}, u32[]{:S(2)}, u32[]{:S(2)}) collective-permute-start(f32[16,16,3,128]{3,0,2,1:T(8,128)} %get-tuple-element.12), channel_id=1, source_target_pairs={{1,0},{2,1},{3,2},{4,3},{5,4},{6,5},{7,6},{8,7},{9,8},{10,9},{11,1... | collective-permute-start | bytes 1179656 | tf_op jit(solution)/shard_map/ppermute | solution.py:17
  33.7 1.9 collective-permute-start.5
  35.6 3.6 %collective-permute-start.6 = (f32[18,1,128]{2,1,0:T(1,128)}, f32[18,1,128]{2,1,0:T(1,128)}, u32[]{:S(2)}, u32[]{:S(2)}) collective-permute-start(f32[18,1,128]{2,1,0:T(1,128)} %get-tuple-element.14), channel_id=1, source_target_pairs={{0,1},{1,2},{2,3},{3,4},{4,5},{5,6},{6,7},{7,8},{8,9},{9,10},{10,1... | collective-permute-start | bytes 27656 | tf_op jit(solution)/shard_map/ppermute | solution.py:15
  39.8 1.7 slice.216
  42.3 1.2 add_divide_fusion.4
  43.5 4.7 %select_maximum_fusion = f32[48,16,18,128]{3,0,2,1:T(8,128)} fusion(f32[16,16,3,128]{3,0,2,1:T(8,128)} %collective-permute-done.1, f32[16,16,3,128]{3,0,2,1:T(8,128)} %collective-permute-done, f32[16,16,18,128]{3,0,2,1:T(8,128)} %slice.216), kind=kLoop, calls=%fused_computation | loop fusion | flops 10616832 | bytes 10223616 | tf_op jit(solution)/shard_map/concatenate | solution.py:39
  48.2 10.9 %fusion.55 = (f32[48,16,16,127]{3,0,2,1:T(8,128)}, f32[48,16,16,127]{3,0,2,1:T(8,128)}) fusion(f32[48,16,18,128]{3,0,2,1:T(8,128)} %select_maximum_fusion), kind=kLoop, calls=%fused_computation.86 | loop fusion | bytes 24969216 | tf_op jit(solution)/shard_map/slice | solution.py:90
  59.1 10.0 %fusion.54 = (f32[48,15,16,128]{3,0,2,1:T(8,128)}, f32[48,15,16,128]{3,0,2,1:T(8,128)}) fusion(f32[48,16,18,128]{3,0,2,1:T(8,128)} %select_maximum_fusion), kind=kLoop, calls=%fused_computation.85 | loop fusion | bytes 23592960 | tf_op jit(solution)/shard_map/slice | solution.py:84
  69.1 1.2 fusion.53
  70.2 1.3 collective-permute-start.7
  71.6 20.4 %fusion.30 = f32[48,48]{1,0:T(8,128)S(1)} fusion(f32[48,16,18,128]{3,0,2,1:T(8,128)} %select_maximum_fusion, f32[48,16,16,127]{3,0,2,1:T(8,128)} %get-tuple-element.10, f32[48,16,16,127]{3,0,2,1:T(8,128)} %get-tuple-element.9, f32[48,15,16,128]{3,0,2,1:T(8,128)} %get-tuple-element.8, f32[48,15,16,128]{3,0,2,1:T(8,128)} %get-tuple-element.7, ...), kind=kOutput, calls=%fused_computation.35 | convolution fusion | flops 932708352 | bytes 51127296 | tf_op jit(solution)/shard_map/axzy,bxzy->ab/dot_general | solution.py:94
  92.1 4.0 %collective-permute-start.3 = (f32[48,1,16,128]{3,0,2,1:T(8,128)S(1)}, f32[48,1,16,128]{3,0,2,1:T(8,128)S(1)}, u32[]{:S(2)}, u32[]{:S(2)}) collective-permute-start(f32[48,1,16,128]{3,0,2,1:T(8,128)S(1)} %get-tuple-element.6), channel_id=1, source_target_pairs={{0,32},{32,64},{64,96},{96,128},{128,160},{160,192},{192,224},{224... | collective-permute-start | bytes 1179656 | tf_op jit(solution)/shard_map/ppermute | solution.py:15
  96.2 1.5 fusion.33
  97.8 7.1 %collective-permute-done.3 = f32[48,1,16,128]{3,0,2,1:T(8,128)S(1)} collective-permute-done((f32[48,1,16,128]{3,0,2,1:T(8,128)S(1)}, f32[48,1,16,128]{3,0,2,1:T(8,128)S(1)}, u32[]{:S(2)}, u32[]{:S(2)}) %collective-permute-start.3) | collective-permute-done | bytes 393248 | tf_op jit(solution)/shard_map/ppermute | solution.py:15
  104.9 1.5 fusion.34
  107.4 1.1 copy.76
  108.6 109.1 %reduce-scatter.2.cloned.1.call-done = f32[1,16,144]{2,1,0:T(8,128)} async-done(((f32[32,16,144]{2,1,0:T(8,128)}), f32[1,16,144]{2,1,0:T(8,128)}) %reduce-scatter.2.cloned.1.call-update) | async-done | bytes 9232 | tf_op jit(solution)/shard_map/reduce_scatter | solution.py:117
  217.6 32.2 %all_gather.3 = f32[32,16,144]{2,1,0:T(8,128)S(1)} all-gather(f32[1,16,144]{2,1,0:T(8,128)} %reduce-scatter.2.cloned.1.call-done), channel_id=1, replica_groups=mesh['grp'=16,'sub'=32] {'sub'}, dimensions={0}, use_global_device_ids=true | all-gather | bytes 304128 | tf_op jit(solution)/shard_map/all_gather | solution.py:118
  (46 shorter events, 7.0 us)
Async XLA Ops:
  6.5 23.5 %copy-start = (f32[16,16,128]{2,1,0:T(8,128)S(1)}, f32[16,16,128]{2,1,0:T(8,128)}, u32[]{:S(2)}) copy-start(f32[16,16,128]{2,1,0:T(8,128)} %param.5) | copy-start | bytes 393220
  6.5 211.1 %reduce-scatter.2.cloned.1.call-start = ((), (), s32[]{:S(2)}) async-start(), calls=%async_computation.1 | async-start | bytes 540672 | tf_op jit(solution)/shard_map/reduce_scatter | solution.py:117
  7.9 23.1 %collective-permute-start.4 = (f32[1,16,128]{2,1,0:T(8,128)}, f32[1,16,128]{2,1,0:T(8,128)S(1)}, u32[]{:S(2)}, u32[]{:S(2)}) collective-permute-start(f32[1,16,128]{2,1,0:T(8,128)} %get-tuple-element.29), channel_id=1, source_target_pairs={{32,0},{64,32},{96,64},{128,96},{160,128},{192,160},{224,192},{256... | collective-permute-start | bytes 24584 | tf_op jit(solution)/shard_map/ppermute | solution.py:17
  9.2 22.4 %collective-permute-start.2 = (f32[1,16,128]{2,1,0:T(8,128)S(1)}, f32[1,16,128]{2,1,0:T(8,128)}, u32[]{:S(2)}, u32[]{:S(2)}) collective-permute-start(f32[1,16,128]{2,1,0:T(8,128)S(1)} %get-tuple-element.30), channel_id=1, source_target_pairs={{0,32},{32,64},{64,96},{96,128},{128,160},{160,192},{192,224},{224... | collective-permute-start | bytes 24584 | tf_op jit(solution)/shard_map/ppermute | solution.py:15
  19.3 24.1 %collective-permute-start = (f32[16,16,3,128]{3,0,2,1:T(8,128)}, f32[16,16,3,128]{3,0,2,1:T(8,128)}, u32[]{:S(2)}, u32[]{:S(2)}) collective-permute-start(f32[16,16,3,128]{3,0,2,1:T(8,128)} %get-tuple-element.11), channel_id=1, source_target_pairs={{0,1},{1,2},{2,3},{3,4},{4,5},{5,6},{6,7},{7,8},{8,9},{9,10},{10,1... | collective-permute-start | bytes 1179656 | tf_op jit(solution)/shard_map/ppermute | solution.py:15
  24.2 19.3 %collective-permute-start.1 = (f32[16,16,3,128]{3,0,2,1:T(8,128)}, f32[16,16,3,128]{3,0,2,1:T(8,128)}, u32[]{:S(2)}, u32[]{:S(2)}) collective-permute-start(f32[16,16,3,128]{3,0,2,1:T(8,128)} %get-tuple-element.12), channel_id=1, source_target_pairs={{1,0},{2,1},{3,2},{4,3},{5,4},{6,5},{7,6},{8,7},{9,8},{10,9},{11,1... | collective-permute-start | bytes 1179656 | tf_op jit(solution)/shard_map/ppermute | solution.py:17
  31.0 0.6 copy-start.1
  33.7 7.9 %collective-permute-start.5 = (f32[18,1,128]{2,1,0:T(1,128)}, f32[18,1,128]{2,1,0:T(1,128)}, u32[]{:S(2)}, u32[]{:S(2)}) collective-permute-start(f32[18,1,128]{2,1,0:T(1,128)} %get-tuple-element.13), channel_id=1, source_target_pairs={{1,0},{2,1},{3,2},{4,3},{5,4},{6,5},{7,6},{8,7},{9,8},{10,9},{11,1... | collective-permute-start | bytes 27656 | tf_op jit(solution)/shard_map/ppermute | solution.py:17
  35.6 6.0 %collective-permute-start.6 = (f32[18,1,128]{2,1,0:T(1,128)}, f32[18,1,128]{2,1,0:T(1,128)}, u32[]{:S(2)}, u32[]{:S(2)}) collective-permute-start(f32[18,1,128]{2,1,0:T(1,128)} %get-tuple-element.14), channel_id=1, source_target_pairs={{0,1},{1,2},{2,3},{3,4},{4,5},{5,6},{6,7},{7,8},{8,9},{9,10},{10,1... | collective-permute-start | bytes 27656 | tf_op jit(solution)/shard_map/ppermute | solution.py:15
  70.2 25.9 %collective-permute-start.7 = (f32[48,1,16,128]{3,0,2,1:T(8,128)S(1)}, f32[48,1,16,128]{3,0,2,1:T(8,128)S(1)}, u32[]{:S(2)}, u32[]{:S(2)}) collective-permute-start(f32[48,1,16,128]{3,0,2,1:T(8,128)S(1)} %get-tuple-element.5), channel_id=1, source_target_pairs={{32,0},{64,32},{96,64},{128,96},{160,128},{192,160},{224,192},{256... | collective-permute-start | bytes 1179656 | tf_op jit(solution)/shard_map/ppermute | solution.py:17
  71.5 35.4 %copy-start.2 = (s32[1,32]{1,0:T(1,128)S(1)}, s32[1,32]{1,0:T(1,128)}, u32[]{:S(2)}) copy-start(s32[1,32]{1,0:T(1,128)} %param.7) | copy-start | bytes 388
  71.6 35.4 %copy-start.3 = (s32[3]{0:T(128)S(1)}, s32[3]{0:T(128)}, u32[]{:S(2)}) copy-start(s32[3]{0:T(128)} %add_add_fusion) | copy-start | bytes 40
  92.1 12.8 %collective-permute-start.3 = (f32[48,1,16,128]{3,0,2,1:T(8,128)S(1)}, f32[48,1,16,128]{3,0,2,1:T(8,128)S(1)}, u32[]{:S(2)}, u32[]{:S(2)}) collective-permute-start(f32[48,1,16,128]{3,0,2,1:T(8,128)S(1)} %get-tuple-element.6), channel_id=1, source_target_pairs={{0,32},{32,64},{64,96},{96,128},{128,160},{160,192},{192,224},{224... | collective-permute-start | bytes 1179656 | tf_op jit(solution)/shard_map/ppermute | solution.py:15
Sparse Core Ops, SparseCore 0:
  108.7 108.9 reduce-scatter.1
where the time goes:
time: 258 us; the launch traced here: 257 us
  waiting for transfers between devices  116 us (45%)
  blocking collectives  32.2 us (12%)
  local copies, waits for them, and re-layouts  31.6 us (12%)
  starting transfers between devices  28.1 us (11%)
  matrix products  23.9 us (9%)
  between operations  14.3 us (6%)
  other arithmetic  11.2 us (4%)
    reduce_scatter x1, waiting for transfers between devices, per_device(): owned = lax.psum_scatter(placed, 'sub', scatter_dimension=0, tiled=True)  109 us
    all_gather x1, blocking collectives, per_device(): gathered = lax.all_gather(owned, 'sub', axis=0, tiled=True)  32.2 us
    dot_general x1, matrix products, per_device(): self_gram = jnp.einsum('axzy,bxzy->ab', centre, applied, precision=highest)  20.4 us
    ppermute x4, starting transfers between devices, extended_2(): lax.ppermute(tail, axis, [(i, (i + 1) % count) for i in range(ends)])  17.7 us
    slice x1, local copies, waits for them, and re-layouts, per_device(): centre[..., 1:]  10.9 us
    ppermute x4, starting transfers between devices, extended_2(): lax.ppermute(head, axis, [((i + 1) % count, i) for i in range(ends)])  10.4 us
    slice x1, local copies, waits for them, and re-layouts, per_device(): centre[:, 1:]  9.96 us
    ppermute x4, waiting for transfers between devices, extended_2(): lax.ppermute(tail, axis, [(i, (i + 1) % count) for i in range(ends)])  7.11 us
  transfers between devices with their start and end apart: 9, of which 2 were waited for; matrix products, arithmetic and copies ran while one was open for 13% of the time, Pallas kernels for 0%

commit v1 on v0

v1 whole, which is shorter than its diff:
```python
import functools

import jax
import jax.numpy as jnp
from jax import lax
from jax.experimental import pallas as pl
from jax.experimental.pallas import tpu as pltpu
from jax.sharding import PartitionSpec as P

MESH = pl.DeviceIdType.MESH
KV = 16
OV = 2
CX = 16
CZ = 16
NY = 128
EXT = CZ + 2 * OV
GROUP = 4
MSG = 24


def harmonic(first_perm, second_perm):
    return 2.0 * first_perm * second_perm / (first_perm + second_perm)


def split(values):
    high = values.astype(jnp.bfloat16)
    low = (values - high.astype(jnp.float32)).astype(jnp.bfloat16)
    return high, low


def stack_split(values):
    pairs = [split(value) for value in values]
    high = jnp.concatenate([pair[0] for pair in pairs], axis=1)
    low = jnp.concatenate([pair[1] for pair in pairs], axis=1)
    return jnp.concatenate([high, low], axis=0)


def gram(first, second):
    return lax.dot_general(
        first, second, (((1,), (1,)), ((), ())), preferred_element_type=jnp.float32
    )


def fold(product):
    return (product[:KV, :KV] + product[:KV, KV:]) + (product[KV:, :KV] + product[KV:, KV:])


def assemble_kernel(n_grp, n_sub, vec, perm, counts, out, z, zup, zdn, xl, xr, xd,
                    pown, pzl, pzu, pxl, pxr, pc, pe, fx, fz, fy, dg, wp1, wp2, wl, wr, msg,
                    load_sem, send_sem, recv_sem, all_send, all_recv):
    s = lax.axis_index("sub")
    g = lax.axis_index("grp")
    up, down = lax.rem(s + 1, n_sub), lax.rem(s + n_sub - 1, n_sub)
    right, left = lax.rem(g + 1, n_grp), lax.rem(g + n_grp - 1, n_grp)

    for a in range(KV):
        pltpu.make_async_copy(
            vec.at[a], z.at[pl.ds(1, CX), pl.ds(1, EXT), a, :], load_sem.at[0]
        ).start()
    pltpu.make_async_copy(perm, pown, load_sem.at[1]).start()

    barrier = pltpu.get_barrier_semaphore()
    for tg in (left, right):
        for ts in (s, up, down):
            pl.semaphore_signal(barrier, inc=1, device_id=(tg, ts), device_id_type=MESH)

    def greet(k, carry):
        pl.semaphore_signal(
            barrier, inc=1, device_id=(g, lax.rem(s + k, n_sub)), device_id_type=MESH
        )
        return carry

    lax.fori_loop(1, n_sub, greet, 0)

    zero_block = jnp.zeros((KV, NY), jnp.float32)
    for r in range(EXT + 2):
        z[0, r] = zero_block
        z[CX + 1, r] = zero_block

    def zero_ends(x, carry):
        z[x, 0] = zero_block
        z[x, EXT + 1] = zero_block
        return carry

    lax.fori_loop(1, CX + 1, zero_ends, 0)

    pl.semaphore_wait(barrier, n_sub - 1 + 6)

    def send(slot, src, dst, tg, ts):
        copy = pltpu.make_async_remote_copy(
            src_ref=src, dst_ref=dst, send_sem=send_sem.at[slot], recv_sem=recv_sem.at[slot],
            device_id=(tg, ts), device_id_type=MESH,
        )
        copy.start()
        return copy

    half = CZ // 2
    perm_copies = [
        send(0, perm.at[:, pl.ds(half, half), :], pzl, g, up),
        send(1, perm.at[:, pl.ds(0, half), :], pzu, g, down),
        send(2, perm.at[CX - 1], pxl, right, s),
        send(3, perm.at[0], pxr, left, s),
        send(4, perm.at[CX - 1, pl.ds(half, half), :], pc.at[0], right, up),
        send(5, perm.at[CX - 1, pl.ds(0, half), :], pc.at[1], right, down),
        send(6, perm.at[0, pl.ds(half, half), :], pc.at[2], left, up),
        send(7, perm.at[0, pl.ds(0, half), :], pc.at[3], left, down),
    ]

    pltpu.make_async_copy(
        z.at[pl.ds(1, CX), pl.ds(1, EXT)], z.at[pl.ds(1, CX), pl.ds(1, EXT)], load_sem.at[0]
    ).wait()
    count = counts[0, 0]
    own_rows = (lax.broadcasted_iota(jnp.int32, (KV, NY), 0) < count).astype(jnp.float32)
    low_keep = own_rows * (s > 0).astype(jnp.float32)
    high_keep = own_rows * (s < n_sub - 1).astype(jnp.float32)

    def keep_of(r):
        return low_keep if r < OV else high_keep if r >= EXT - OV else own_rows

    def mask_ends(x, carry):
        for r in (0, 1, 2, EXT - 2, EXT - 1):
            z[x, r + 1] = z[x, r + 1] * keep_of(r)
        return carry

    lax.fori_loop(1, CX + 1, mask_ends, 0)
    for x in (1, CX):
        for r in range(3, EXT - 2):
            z[x, r + 1] = z[x, r + 1] * own_rows

    all_slots = pl.ds(1, EXT)
    vec_copies = [
        send(8, z.at[pl.ds(1, CX), pl.ds(1, 3)], zup, g, down),
        send(9, z.at[pl.ds(1, CX), pl.ds(EXT - 1, 2)], zdn, g, up),
        send(10, z.at[1, all_slots], xr, left, s),
        send(11, z.at[CX, all_slots], xl, right, s),
        send(12, z.at[CX, pl.ds(EXT - 3, 4)], xd.at[0], right, up),
        send(13, z.at[CX, pl.ds(1, 4)], xd.at[1], right, down),
        send(14, z.at[1, pl.ds(EXT - 3, 4)], xd.at[2], left, up),
        send(15, z.at[1, pl.ds(1, 4)], xd.at[3], left, down),
    ]

    pltpu.make_async_copy(perm, pown, load_sem.at[1]).wait()
    for copy in perm_copies:
        copy.wait_recv()
    at_low, at_high = s == 0, s == n_sub - 1
    at_left, at_right = g == 0, g == n_grp - 1

    def fill_perm(x, carry):
        own = pown[x]
        pe[x + 1, 3 : 3 + CZ] = own
        pe[x + 1, 0:3] = jnp.where(
            at_low, jnp.broadcast_to(own[0:1], (3, NY)), pzl[x, half - 3 : half]
        )
        pe[x + 1, 3 + CZ : 6 + CZ] = jnp.where(
            at_high, jnp.broadcast_to(own[CZ - 1 : CZ], (3, NY)), pzu[x, 0:3]
        )
        return carry

    lax.fori_loop(0, CX, fill_perm, 0)
    for edge, at_edge, own_x, face, low, high in (
        (0, at_left, 1, pxl, 0, 1), (CX + 1, at_right, CX, pxr, 2, 3)
    ):
        pe[edge, 3 : 3 + CZ] = jnp.where(at_edge, pe[own_x, 3 : 3 + CZ], face[...])
        pe[edge, 1:3] = jnp.where(
            at_edge, pe[own_x, 1:3],
            jnp.where(at_low, face[0:1], pc[low, half - 2 : half]),
        )
        pe[edge, 3 + CZ : 5 + CZ] = jnp.where(
            at_edge, pe[own_x, 3 + CZ : 5 + CZ],
            jnp.where(at_high, face[CZ - 1 : CZ], pc[high, 0:2]),
        )

    lane = lax.broadcasted_iota(jnp.int32, (EXT, NY), 1)

    fx[0] = harmonic(pe[0, 1 : 1 + EXT], pe[1, 1 : 1 + EXT])

    def coefficients(x, carry):
        own = pe[x + 1, 1 : 1 + EXT]
        right_face = harmonic(own, pe[x + 2, 1 : 1 + EXT])
        z_faces = harmonic(pe[x + 1, 0 : 1 + EXT], pe[x + 1, 1 : 2 + EXT])
        fx[x + 1] = right_face
        fz[x] = z_faces
        upward = harmonic(own, pltpu.roll(own, NY - 1, 1))
        coupling = jnp.where(lane == NY - 1, 0.0, upward)
        fy[x] = coupling
        ends = jnp.where(lane == NY - 1, own, upward) + jnp.where(
            lane == 0, own, pltpu.roll(upward, 1, 1)
        )
        dg[x] = (fx[x] + right_face) + (fz[x, 0:EXT] + fz[x, 1 : 1 + EXT]) + ends
        return carry

    lax.fori_loop(0, CX, coefficients, 0)

    not_high = 1.0 - at_high.astype(jnp.float32)

    def column(x, total):
        held = {}
        for first in range(0, EXT, GROUP):
            mine, applied = [], []
            for r in range(first, first + GROUP):
                here = z[x + 1, r + 1]
                along = fy[x, r : r + 1, :]
                result = dg[x, r : r + 1, :] * here
                result = result - fx[x, r : r + 1, :] * z[x, r + 1]
                result = result - fx[x + 1, r : r + 1, :] * z[x + 2, r + 1]
                result = result - fz[x, r : r + 1, :] * z[x + 1, r]
                result = result - fz[x, r + 1 : r + 2, :] * z[x + 1, r + 2]
                result = result - along * pltpu.roll(here, NY - 1, 1)
                result = result - pltpu.roll(along * here, 1, 1)
                mine.append(here)
                applied.append(result)
                if r in (2, 3, EXT - 4, EXT - 3):
                    held[r] = result
            total = total + gram(stack_split(mine), stack_split(applied))
        face = fz[x, EXT - 2 : EXT - 1, :]
        lower = [
            held[EXT - 4],
            held[EXT - 3] + face * z[x + 1, EXT - 1],
            -(face * not_high) * z[x + 1, EXT - 2],
        ]
        wp1[x] = stack_split(lower)
        wp2[x] = stack_split([held[2], held[3]])
        return total

    total = lax.fori_loop(0, CX, column, jnp.zeros((2 * KV, 2 * KV), jnp.float32))

    left_on = 1.0 - at_left.astype(jnp.float32)
    right_on = 1.0 - at_right.astype(jnp.float32)
    for target, on, row, coef in ((wl, left_on, 1, 0), (wr, right_on, CX, CX)):
        target[...] = stack_split(
            [-(fx[coef, r : r + 1, :] * on) * z[row, r + 1] for r in range(EXT)]
        )

    row_keep = lax.broadcasted_iota(jnp.int32, (KV, KV), 0) < count
    col_keep = lax.broadcasted_iota(jnp.int32, (KV, KV), 1) < count
    blocks = {4: jnp.where(row_keep & col_keep, fold(total), 0.0)}

    vec_copies[0].wait_recv()

    def upper_pair(x, carry):
        theirs = stack_split([zup[x, 0], zup[x, 1], zup[x, 2]])
        return carry[0] + gram(wp1[x], theirs), carry[1] + gram(theirs, wp1[x])

    zeros = jnp.zeros((2 * KV, 2 * KV), jnp.float32)
    straight, turned = lax.fori_loop(0, CX, upper_pair, (zeros, zeros))
    blocks[5] = jnp.where(row_keep, fold(straight), 0.0)
    blocks[9] = jnp.where(col_keep, fold(turned), 0.0)

    vec_copies[1].wait_recv()

    def lower_pair(x, carry):
        theirs = stack_split([zdn[x, 0], zdn[x, 1]])
        return carry[0] + gram(wp2[x], theirs), carry[1] + gram(theirs, wp2[x])

    straight, turned = lax.fori_loop(0, CX, lower_pair, (zeros, zeros))
    blocks[3] = jnp.where(row_keep, fold(straight), 0.0)
    blocks[10] = jnp.where(col_keep, fold(turned), 0.0)

    for copy in vec_copies[2:]:
        copy.wait_recv()
    for base, weight, face, low, high in ((0, wl, xl, 0, 1), (6, wr, xr, 2, 3)):
        theirs = stack_split([face[r] for r in range(EXT)])
        blocks[base + 1] = jnp.where(row_keep, fold(gram(weight[...], theirs)), 0.0)
        theirs = stack_split([xd[low, r] for r in range(4)])
        blocks[base] = jnp.where(row_keep, fold(gram(weight[:, : 4 * NY], theirs)), 0.0)
        theirs = stack_split([xd[high, r] for r in range(4)])
        blocks[base + 2] = jnp.where(
            row_keep, fold(gram(weight[:, (EXT - 4) * NY :], theirs)), 0.0
        )

    msg[0:KV, :] = jnp.concatenate([blocks[i] for i in range(8)], axis=1)
    half_v = KV // 2
    gap = jnp.zeros((half_v, KV), jnp.float32)
    parts = [blocks[8][:half_v], blocks[8][half_v:], gap, blocks[9][:half_v], blocks[9][half_v:],
             blocks[10][:half_v], blocks[10][half_v:], gap]
    msg[KV:, :] = jnp.concatenate(parts, axis=1)

    def share(k, carry):
        pltpu.make_async_remote_copy(
            src_ref=msg, dst_ref=out.at[s], send_sem=all_send, recv_sem=all_recv,
            device_id=(g, lax.rem(s + k, n_sub)), device_id_type=MESH,
        ).start()
        return carry

    lax.fori_loop(1, n_sub, share, 0)
    own_copy = pltpu.make_async_copy(msg, out.at[s], load_sem.at[2])
    own_copy.start()
    for copy in perm_copies + vec_copies:
        copy.wait_send()
    own_copy.wait()
    rest = out.at[pl.ds(0, n_sub - 1)]
    pltpu.make_async_copy(rest, rest, all_recv).wait()
    pltpu.make_async_copy(rest, rest, all_send).wait()


def place_kernel(n_sub, ownership, gathered, out):
    lane = lax.broadcasted_iota(jnp.int32, (KV // 2, NY), 1)
    from_below = (lane >= 3 * KV) & (lane < 4 * KV)
    from_above = (lane >= 5 * KV) & (lane < 6 * KV)
    half_v = KV // 2

    def place(j, carry):
        s = ownership[0, j]
        below = gathered[jnp.maximum(s - 1, 0), KV:, :]
        above = gathered[jnp.minimum(s + 1, n_sub - 1), KV:, :]
        below = jnp.where(s > 0, below, 0.0)
        above = jnp.where(s < n_sub - 1, above, 0.0)
        extra = gathered[s, KV:, :]
        for part in range(2):
            shift = NY - part * KV
            if part:
                below = pltpu.roll(below, shift, 1)
                above = pltpu.roll(above, shift, 1)
                extra = pltpu.roll(extra, shift, 1)
            rows = pl.ds(part * half_v, half_v)
            main = gathered[s, rows, :]
            main = main + jnp.where(from_below, below, 0.0) + jnp.where(from_above, above, 0.0)
            out[0, j, rows, 0:NY] = main
            out[0, j, rows, NY:] = extra[:, :KV]
        return carry

    lax.fori_loop(0, n_sub, place, 0)


def per_device(n_grp, n_sub, vectors, permeability, counts, ownership):
    f32, bf16 = jnp.float32, jnp.bfloat16
    vmem = pltpu.VMEM
    gathered = pl.pallas_call(
        functools.partial(assemble_kernel, n_grp, n_sub),
        out_shape=jax.ShapeDtypeStruct((n_sub, MSG, NY), f32),
        in_specs=[
            pl.BlockSpec(memory_space=pl.ANY),
            pl.BlockSpec(memory_space=pl.ANY),
            pl.BlockSpec(memory_space=pltpu.SMEM),
        ],
        out_specs=pl.BlockSpec(memory_space=pl.ANY),
        scratch_shapes=[
            vmem((CX + 2, EXT + 2, KV, NY), f32),
            vmem((CX, 3, KV, NY), f32),
            vmem((CX, 2, KV, NY), f32),
            vmem((EXT, KV, NY), f32),
            vmem((EXT, KV, NY), f32),
            vmem((4, 4, KV, NY), f32),
            vmem((CX, CZ, NY), f32),
            vmem((CX, CZ // 2, NY), f32),
            vmem((CX, CZ // 2, NY), f32),
            vmem((CZ, NY), f32),
            vmem((CZ, NY), f32),
            vmem((4, CZ // 2, NY), f32),
            vmem((CX + 2, EXT + 4, NY), f32),
            vmem((CX + 1, EXT, NY), f32),
            vmem((CX, EXT + 1, NY), f32),
            vmem((CX, EXT, NY), f32),
            vmem((CX, EXT, NY), f32),
            vmem((CX, 2 * KV, 3 * NY), bf16),
            vmem((CX, 2 * KV, 2 * NY), bf16),
            vmem((2 * KV, EXT * NY), bf16),
            vmem((2 * KV, EXT * NY), bf16),
            vmem((MSG, NY), f32),
            pltpu.SemaphoreType.DMA((3,)),
            pltpu.SemaphoreType.DMA((16,)),
            pltpu.SemaphoreType.DMA((16,)),
            pltpu.SemaphoreType.DMA,
            pltpu.SemaphoreType.DMA,
        ],
        compiler_params=pltpu.CompilerParams(
            collective_id=0, has_side_effects=True, vmem_limit_bytes=32 << 20
        ),
    )(vectors, permeability, counts)
    return pl.pallas_call(
        functools.partial(place_kernel, n_sub),
        out_shape=jax.ShapeDtypeStruct((1, n_sub, KV, 9 * KV), f32),
        in_specs=[
            pl.BlockSpec(memory_space=pltpu.SMEM),
            pl.BlockSpec(memory_space=pltpu.VMEM),
        ],
        out_specs=pl.BlockSpec(memory_space=pltpu.VMEM),
    )(ownership, gathered)


def solution(mesh):
    in_specs = (P(None, "grp", "sub", None), P("grp", "sub", None), P("grp", "sub"), P("grp", None))
    out_specs = P("grp", None, None, None)
    return jax.shard_map(
        functools.partial(per_device, mesh.shape["grp"], mesh.shape["sub"]),
        mesh=mesh, in_specs=in_specs, out_specs=out_specs, check_vma=False,
    )
```

time: 258 us -> 65.5 us (0.25)
  waiting for transfers between devices: 116 us -> 0 us
  Pallas kernels: 0 us -> 61.3 us
  blocking collectives: 32.2 us -> 0 us
  local copies, waits for them, and re-layouts: 31.6 us -> 3.32 us
  starting transfers between devices: 28.1 us -> 0 us
  matrix products: 23.9 us -> 0 us
  between operations: 14.3 us -> 0.72 us
  other arithmetic: 11.2 us -> 0 us
    reduce_scatter x1 -> x0, waiting for transfers between devices: 109 us -> none  [per_device(): owned = lax.psum_scatter(placed, 'sub', scatter_dimension=0, tiled=True)]
    pallas_call x0 -> x2, Pallas kernels: none -> 61.3 us  [the longest x1 57.1 us: per_device(): pl.pallas_call(functools.partial(assemble_kernel, n_grp, n_sub), out_shap...]
    all_gather x1 -> x0, blocking collectives: 32.2 us -> none  [per_device(): gathered = lax.all_gather(owned, 'sub', axis=0, tiled=True)]
    ppermute x8 -> x0, starting transfers between devices: 28.1 us -> none  [the longest x4 17.7 us: extended_2(): lax.ppermute(tail, axis, [(i, (i + 1) % count) for i in range(ends)])]
    slice x14 -> x0, local copies, waits for them, and re-layouts: 27.8 us -> none  [the longest x1 10.9 us: per_device(): centre[..., 1:]]
    dot_general x4 -> x0, matrix products: 23.9 us -> none  [the longest x1 20.4 us: per_device(): self_gram = jnp.einsum('axzy,bxzy->ab', centre, applied, precision=highest)]
    ppermute x8 -> x0, waiting for transfers between devices: 7.12 us -> none  [the longest x4 7.11 us: extended_2(): lax.ppermute(tail, axis, [(i, (i + 1) % count) for i in range(ends)])]
    concatenate x1 -> x0, other arithmetic: 4.67 us -> none  [stack_vectors(): return jnp.concatenate([below_full, middle, above_full], axis=0)]
  transfers between devices with their start and end apart: 9 -> 0, of which waited for: 2 -> 0; matrix products, arithmetic and copies ran while one was open for 13% -> 0% of each run, Pallas kernels for 0% -> 0%
where the time goes in v1:
time: 65.5 us; the launch traced here: 65.3 us
  Pallas kernels  61.3 us (94%)
  local copies, waits for them, and re-layouts  3.32 us (5%)
  between operations  0.72 us (1%)
    pallas_call x1, Pallas kernels, per_device(): pl.pallas_call(functools.partial(assemble_kernel, n_grp, n_sub), out_shap...  57.1 us
    pallas_call x1, Pallas kernels, per_device(): pl.pallas_call(functools.partial(place_kernel, n_sub), out_shape=jax.Shap...  4.16 us
    unnamed x5, local copies, waits for them, and re-layouts  3.32 us

profile of v1, /device:TPU:1, one launch (start us, length us, event | category | flops | bytes accessed | tf_op | source)
XLA Modules:
  0.0 65.3 jit_solution(15696095825785585299)
XLA Ops:
  0.0 0.0 copy-start.1
  0.7 2.6 %copy.5.vec = f32[16,16,20,128]{3,2,1,0:T(8,128)S(1)} copy(f32[16,16,20,128]{3,1,2,0:T(8,128)} %param.4) | data formatting | bytes 5242880 | tf_op args[0]
  3.3 0.0 copy-done.1
  3.3 57.1 %shard_map.46.gathered = f32[32,24,128]{2,1,0:T(8,128)S(1)} custom-call(f32[16,16,20,128]{3,2,1,0:T(8,128)S(1)} %copy.5.vec, f32[16,16,128]{2,1,0:T(8,128)S(1)} %copy-done.1, s32[1,1]{1,0:T(1,128)S(6)} %copy.6.counts), custom_call_target="tpu_custom_call" | custom-call | tf_op jit(solution)/shard_map/pallas_call | solution.py:328
  60.4 0.0 copy-start
  60.5 0.7 %copy-done = f32[32,24,128]{2,1,0:T(8,128)} copy-done((f32[32,24,128]{2,1,0:T(8,128)}, f32[32,24,128]{2,1,0:T(8,128)S(1)}, u32[]{:S(2)}) %copy-start) | copy-done | bytes 393240
  61.2 4.2 %shard_map.47 = f32[1,32,16,144]{3,2,1,0:T(8,128)} custom-call(s32[1,32]{1,0:T(1,128)} %ownership.1, f32[32,24,128]{2,1,0:T(8,128)} %copy-done), custom_call_target="tpu_custom_call" | custom-call | tf_op jit(solution)/shard_map/pallas_call | solution.py:370
Async XLA Ops:
  0.0 3.3 %copy-start.1 = (f32[16,16,128]{2,1,0:T(8,128)S(1)}, f32[16,16,128]{2,1,0:T(8,128)}, u32[]{:S(2)}) copy-start(f32[16,16,128]{2,1,0:T(8,128)} %perm.1) | copy-start | bytes 393220
  60.4 0.7 %copy-start = (f32[32,24,128]{2,1,0:T(8,128)}, f32[32,24,128]{2,1,0:T(8,128)S(1)}, u32[]{:S(2)}) copy-start(f32[32,24,128]{2,1,0:T(8,128)S(1)} %shard_map.46.gathered) | copy-start | bytes 1179652

commit v2 on v1

--- a/solution.py
+++ b/solution.py
@@ -45,17 +45,20 @@
     return (product[:KV, :KV] + product[:KV, KV:]) + (product[KV:, :KV] + product[KV:, KV:])
 
 
-def assemble_kernel(n_grp, n_sub, vec, perm, counts, out, z, zup, zdn, xl, xr, xd,
-                    pown, pzl, pzu, pxl, pxr, pc, pe, fx, fz, fy, dg, wp1, wp2, wl, wr, msg,
-                    load_sem, send_sem, recv_sem, all_send, all_recv):
+def assemble_kernel(n_grp, n_sub, vec, perm, counts, ownership, out, z, zup, zdn, xl, xr, xd,
+                    pown, pzl, pzu, pxl, pxr, pc, pe, fx, fz, fy, dg, wp1, wp2, wl, wr, pool,
+                    load_sem, send_sem, recv_sem, all_send, all_recv, pair_send, pair_recv, known):
     s = lax.axis_index("sub")
     g = lax.axis_index("grp")
     up, down = lax.rem(s + 1, n_sub), lax.rem(s + n_sub - 1, n_sub)
+    chip, core = s // 2, lax.rem(s, 2)
+    n_chip = n_sub // 2
+    mate = chip * 2 + 1 - core
     right, left = lax.rem(g + 1, n_grp), lax.rem(g + n_grp - 1, n_grp)
 
     for a in range(KV):
         pltpu.make_async_copy(
-            vec.at[a], z.at[pl.ds(1, CX), pl.ds(1, EXT), a, :], load_sem.at[0]
+            vec.at[a], z.at[pl.ds(1, EXT), pl.ds(1, CX), a, :], load_sem.at[0]
         ).start()
     pltpu.make_async_copy(perm, pown, load_sem.at[1]).start()
 
@@ -63,28 +66,29 @@
     for tg in (left, right):
         for ts in (s, up, down):
             pl.semaphore_signal(barrier, inc=1, device_id=(tg, ts), device_id_type=MESH)
-
-    def greet(k, carry):
-        pl.semaphore_signal(
-            barrier, inc=1, device_id=(g, lax.rem(s + k, n_sub)), device_id_type=MESH
-        )
-        return carry
-
-    lax.fori_loop(1, n_sub, greet, 0)
+    for ts in (up, down):
+        pl.semaphore_signal(barrier, inc=1, device_id=(g, ts), device_id_type=MESH)
 
     zero_block = jnp.zeros((KV, NY), jnp.float32)
     for r in range(EXT + 2):
-        z[0, r] = zero_block
-        z[CX + 1, r] = zero_block
+        z[r, 0] = zero_block
+        z[r, CX + 1] = zero_block
 
     def zero_ends(x, carry):
-        z[x, 0] = zero_block
-        z[x, EXT + 1] = zero_block
+        z[0, x] = zero_block
+        z[EXT + 1, x] = zero_block
         return carry
 
     lax.fori_loop(1, CX + 1, zero_ends, 0)
 
-    pl.semaphore_wait(barrier, n_sub - 1 + 6)
+    pl.semaphore_wait(barrier, 8)
+
+    def tell(step):
+        reach = 1 << step
+        for ts in (lax.rem(s + reach, n_sub), lax.rem(s + n_sub - reach, n_sub)):
+            pl.semaphore_signal(known.at[step], inc=1, device_id=(g, ts), device_id_type=MESH)
+
+    tell(0)
 
     def send(slot, src, dst, tg, ts):
         copy = pltpu.make_async_remote_copy(
@@ -107,7 +111,7 @@
     ]
 
     pltpu.make_async_copy(
-        z.at[pl.ds(1, CX), pl.ds(1, EXT)], z.at[pl.ds(1, CX), pl.ds(1, EXT)], load_sem.at[0]
+        z.at[pl.ds(1, EXT), pl.ds(1, CX)], z.at[pl.ds(1, EXT), pl.ds(1, CX)], load_sem.at[0]
     ).wait()
     count = counts[0, 0]
     own_rows = (lax.broadcasted_iota(jnp.int32, (KV, NY), 0) < count).astype(jnp.float32)
@@ -119,29 +123,35 @@
 
     def mask_ends(x, carry):
         for r in (0, 1, 2, EXT - 2, EXT - 1):
-            z[x, r + 1] = z[x, r + 1] * keep_of(r)
+            z[r + 1, x] = z[r + 1, x] * keep_of(r)
         return carry
 
     lax.fori_loop(1, CX + 1, mask_ends, 0)
     for x in (1, CX):
         for r in range(3, EXT - 2):
-            z[x, r + 1] = z[x, r + 1] * own_rows
-
+            z[r + 1, x] = z[r + 1, x] * own_rows
+
+    for copy in perm_copies:
+        copy.wait_send()
     all_slots = pl.ds(1, EXT)
     vec_copies = [
-        send(8, z.at[pl.ds(1, CX), pl.ds(1, 3)], zup, g, down),
-        send(9, z.at[pl.ds(1, CX), pl.ds(EXT - 1, 2)], zdn, g, up),
-        send(10, z.at[1, all_slots], xr, left, s),
-        send(11, z.at[CX, all_slots], xl, right, s),
-        send(12, z.at[CX, pl.ds(EXT - 3, 4)], xd.at[0], right, up),
-        send(13, z.at[CX, pl.ds(1, 4)], xd.at[1], right, down),
-        send(14, z.at[1, pl.ds(EXT - 3, 4)], xd.at[2], left, up),
-        send(15, z.at[1, pl.ds(1, 4)], xd.at[3], left, down),
+        send(8, z.at[pl.ds(1, 3), pl.ds(1, CX)], zup, g, down),
+        send(9, z.at[pl.ds(EXT - 1, 2), pl.ds(1, CX)], zdn, g, up),
+        send(10, z.at[all_slots, 1], xr, left, s),
+        send(11, z.at[all_slots, CX], xl, right, s),
+        send(12, z.at[pl.ds(EXT - 3, 4), CX], xd.at[0], right, up),
+        send(13, z.at[pl.ds(1, 4), CX], xd.at[1], right, down),
+        send(14, z.at[pl.ds(EXT - 3, 4), 1], xd.at[2], left, up),
+        send(15, z.at[pl.ds(1, 4), 1], xd.at[3], left, down),
     ]
 
+    pl.semaphore_wait(known.at[0], 2)
+    tell(1)
     pltpu.make_async_copy(perm, pown, load_sem.at[1]).wait()
     for copy in perm_copies:
         copy.wait_recv()
+    pl.semaphore_wait(known.at[1], 2)
+    tell(2)
     at_low, at_high = s == 0, s == n_sub - 1
     at_left, at_right = g == 0, g == n_grp - 1
 
@@ -198,13 +208,13 @@
         for first in range(0, EXT, GROUP):
             mine, applied = [], []
             for r in range(first, first + GROUP):
-                here = z[x + 1, r + 1]
+                here = z[r + 1, x + 1]
                 along = fy[x, r : r + 1, :]
                 result = dg[x, r : r + 1, :] * here
-                result = result - fx[x, r : r + 1, :] * z[x, r + 1]
-                result = result - fx[x + 1, r : r + 1, :] * z[x + 2, r + 1]
-                result = result - fz[x, r : r + 1, :] * z[x + 1, r]
-                result = result - fz[x, r + 1 : r + 2, :] * z[x + 1, r + 2]
+                result = result - fx[x, r : r + 1, :] * z[r + 1, x]
+                result = result - fx[x + 1, r : r + 1, :] * z[r + 1, x + 2]
+                result = result - fz[x, r : r + 1, :] * z[r, x + 1]
+                result = result - fz[x, r + 1 : r + 2, :] * z[r + 2, x + 1]
                 result = result - along * pltpu.roll(here, NY - 1, 1)
                 result = result - pltpu.roll(along * here, 1, 1)
                 mine.append(here)
@@ -215,20 +225,23 @@
         face = fz[x, EXT - 2 : EXT - 1, :]
         lower = [
             held[EXT - 4],
-            held[EXT - 3] + face * z[x + 1, EXT - 1],
-            -(face * not_high) * z[x + 1, EXT - 2],
+            held[EXT - 3] + face * z[EXT - 1, x + 1],
+            -(face * not_high) * z[EXT - 2, x + 1],
         ]
         wp1[x] = stack_split(lower)
         wp2[x] = stack_split([held[2], held[3]])
         return total
 
-    total = lax.fori_loop(0, CX, column, jnp.zeros((2 * KV, 2 * KV), jnp.float32))
+    total = lax.fori_loop(0, CX // 2, column, jnp.zeros((2 * KV, 2 * KV), jnp.float32))
+    pl.semaphore_wait(known.at[2], 2)
+    tell(3)
+    total = lax.fori_loop(CX // 2, CX, column, total)
 
     left_on = 1.0 - at_left.astype(jnp.float32)
     right_on = 1.0 - at_right.astype(jnp.float32)
     for target, on, row, coef in ((wl, left_on, 1, 0), (wr, right_on, CX, CX)):
         target[...] = stack_split(
-            [-(fx[coef, r : r + 1, :] * on) * z[row, r + 1] for r in range(EXT)]
+            [-(fx[coef, r : r + 1, :] * on) * z[r + 1, row] for r in range(EXT)]
         )
 
     row_keep = lax.broadcasted_iota(jnp.int32, (KV, KV), 0) < count
@@ -238,7 +251,7 @@
     vec_copies[0].wait_recv()
 
     def upper_pair(x, carry):
-        theirs = stack_split([zup[x, 0], zup[x, 1], zup[x, 2]])
+        theirs = stack_split([zup[0, x], zup[1, x], zup[2, x]])
         return carry[0] + gram(wp1[x], theirs), carry[1] + gram(theirs, wp1[x])
 
     zeros = jnp.zeros((2 * KV, 2 * KV), jnp.float32)
@@ -249,7 +262,7 @@
     vec_copies[1].wait_recv()
 
     def lower_pair(x, carry):
-        theirs = stack_split([zdn[x, 0], zdn[x, 1]])
+        theirs = stack_split([zdn[0, x], zdn[1, x]])
         return carry[0] + gram(wp2[x], theirs), carry[1] + gram(theirs, wp2[x])
 
     straight, turned = lax.fori_loop(0, CX, lower_pair, (zeros, zeros))
@@ -268,6 +281,7 @@
             row_keep, fold(gram(weight[:, (EXT - 4) * NY :], theirs)), 0.0
         )
 
+    msg = pool.at[chip, core]
     msg[0:KV, :] = jnp.concatenate([blocks[i] for i in range(8)], axis=1)
     half_v = KV // 2
     gap = jnp.zeros((half_v, KV), jnp.float32)
@@ -275,69 +289,76 @@
              blocks[10][:half_v], blocks[10][half_v:], gap]
     msg[KV:, :] = jnp.concatenate(parts, axis=1)
 
+    pl.semaphore_wait(known.at[3], 2)
+
     def share(k, carry):
         pltpu.make_async_remote_copy(
-            src_ref=msg, dst_ref=out.at[s], send_sem=all_send, recv_sem=all_recv,
-            device_id=(g, lax.rem(s + k, n_sub)), device_id_type=MESH,
+            src_ref=msg, dst_ref=msg, send_sem=all_send, recv_sem=all_recv,
+            device_id=(g, lax.rem(s + n_sub // 2 + 2 * k, n_sub)), device_id_type=MESH,
         ).start()
         return carry
 
-    lax.fori_loop(1, n_sub, share, 0)
-    own_copy = pltpu.make_async_copy(msg, out.at[s], load_sem.at[2])
-    own_copy.start()
-    for copy in perm_copies + vec_copies:
+    lax.fori_loop(0, n_chip // 2, share, 0)
+    lax.fori_loop(n_chip // 2 + 1, n_chip, share, 0)
+    for copy in vec_copies:
         copy.wait_send()
-    own_copy.wait()
-    rest = out.at[pl.ds(0, n_sub - 1)]
+    rest = pool.at[pl.ds(0, n_chip - 1), 0]
     pltpu.make_async_copy(rest, rest, all_recv).wait()
-    pltpu.make_async_copy(rest, rest, all_send).wait()
-
-
-def place_kernel(n_sub, ownership, gathered, out):
-    lane = lax.broadcasted_iota(jnp.int32, (KV // 2, NY), 1)
+    mine = pool.at[:, core]
+    pair = pltpu.make_async_remote_copy(
+        src_ref=mine, dst_ref=mine, send_sem=pair_send, recv_sem=pair_recv,
+        device_id=(g, mate), device_id_type=MESH,
+    )
+    pair.start()
+    pair.wait_recv()
+
+    lane = lax.broadcasted_iota(jnp.int32, (half_v, NY), 1)
     from_below = (lane >= 3 * KV) & (lane < 4 * KV)
     from_above = (lane >= 5 * KV) & (lane < 6 * KV)
-    half_v = KV // 2
 
     def place(j, carry):
-        s = ownership[0, j]
-        below = gathered[jnp.maximum(s - 1, 0), KV:, :]
-        above = gathered[jnp.minimum(s + 1, n_sub - 1), KV:, :]
-        below = jnp.where(s > 0, below, 0.0)
-        above = jnp.where(s < n_sub - 1, above, 0.0)
-        extra = gathered[s, KV:, :]
-        for part in range(2):
-            shift = NY - part * KV
-            if part:
-                below = pltpu.roll(below, shift, 1)
-                above = pltpu.roll(above, shift, 1)
-                extra = pltpu.roll(extra, shift, 1)
-            rows = pl.ds(part * half_v, half_v)
-            main = gathered[s, rows, :]
-            main = main + jnp.where(from_below, below, 0.0) + jnp.where(from_above, above, 0.0)
-            out[0, j, rows, 0:NY] = main
-            out[0, j, rows, NY:] = extra[:, :KV]
-        return carry
-
-    lax.fori_loop(0, n_sub, place, 0)
+        row = ownership[0, j]
+        before, after = jnp.maximum(row - 1, 0), jnp.minimum(row + 1, n_sub - 1)
+        below = pool[before // 2, lax.rem(before, 2), KV:, :]
+        above = pool[after // 2, lax.rem(after, 2), KV:, :]
+        extra = pool[row // 2, lax.rem(row, 2), KV:, :]
+        added = jnp.where(from_below & (row > 0), below, 0.0)
+        added = added + jnp.where(from_above & (row < n_sub - 1), above, 0.0)
+        top = pool[row // 2, lax.rem(row, 2), :half_v, :]
+        bottom = pool[row // 2, lax.rem(row, 2), half_v:KV, :]
+        shift = NY - KV
+        below = pltpu.roll(below, shift, 1)
+        above = pltpu.roll(above, shift, 1)
+        out[0, j, :half_v, NY:] = extra[:, :KV]
+        out[0, j, half_v:, NY:] = pltpu.roll(extra, shift, 1)[:, :KV]
+        out[0, j, :half_v, 0:NY] = top + added
+        added = jnp.where(from_below & (row > 0), below, 0.0)
+        added = added + jnp.where(from_above & (row < n_sub - 1), above, 0.0)
+        out[0, j, half_v:, 0:NY] = bottom + added
+        return carry
+
+    lax.fori_loop(0, n_sub, place, 0, unroll=8)
+    pair.wait_send()
+    pltpu.make_async_copy(rest, rest, all_send).wait()
 
 
 def per_device(n_grp, n_sub, vectors, permeability, counts, ownership):
     f32, bf16 = jnp.float32, jnp.bfloat16
     vmem = pltpu.VMEM
-    gathered = pl.pallas_call(
+    return pl.pallas_call(
         functools.partial(assemble_kernel, n_grp, n_sub),
-        out_shape=jax.ShapeDtypeStruct((n_sub, MSG, NY), f32),
+        out_shape=jax.ShapeDtypeStruct((1, n_sub, KV, 9 * KV), f32),
         in_specs=[
             pl.BlockSpec(memory_space=pl.ANY),
             pl.BlockSpec(memory_space=pl.ANY),
             pl.BlockSpec(memory_space=pltpu.SMEM),
+            pl.BlockSpec(memory_space=pltpu.SMEM),
         ],
-        out_specs=pl.BlockSpec(memory_space=pl.ANY),
+        out_specs=pl.BlockSpec(memory_space=pltpu.VMEM),
         scratch_shapes=[
-            vmem((CX + 2, EXT + 2, KV, NY), f32),
-            vmem((CX, 3, KV, NY), f32),
-            vmem((CX, 2, KV, NY), f32),
+            vmem((EXT + 2, CX + 2, KV, NY), f32),
+            vmem((3, CX, KV, NY), f32),
+            vmem((2, CX, KV, NY), f32),
             vmem((EXT, KV, NY), f32),
             vmem((EXT, KV, NY), f32),
             vmem((4, 4, KV, NY), f32),
@@ -356,26 +377,20 @@
             vmem((CX, 2 * KV, 2 * NY), bf16),
             vmem((2 * KV, EXT * NY), bf16),
             vmem((2 * KV, EXT * NY), bf16),
-            vmem((MSG, NY), f32),
-            pltpu.SemaphoreType.DMA((3,)),
+            vmem((n_sub // 2, 2, MSG, NY), f32),
+            pltpu.SemaphoreType.DMA((2,)),
             pltpu.SemaphoreType.DMA((16,)),
             pltpu.SemaphoreType.DMA((16,)),
             pltpu.SemaphoreType.DMA,
             pltpu.SemaphoreType.DMA,
+            pltpu.SemaphoreType.DMA,
+            pltpu.SemaphoreType.DMA,
+            pltpu.SemaphoreType.REGULAR((4,)),
         ],
         compiler_params=pltpu.CompilerParams(
-            collective_id=0, has_side_effects=True, vmem_limit_bytes=32 << 20
+            collective_id=0, has_side_effects=True, vmem_limit_bytes=58 << 20
         ),
-    )(vectors, permeability, counts)
-    return pl.pallas_call(
-        functools.partial(place_kernel, n_sub),
-        out_shape=jax.ShapeDtypeStruct((1, n_sub, KV, 9 * KV), f32),
-        in_specs=[
-            pl.BlockSpec(memory_space=pltpu.SMEM),
-            pl.BlockSpec(memory_space=pltpu.VMEM),
-        ],
-        out_specs=pl.BlockSpec(memory_space=pltpu.VMEM),
-    )(ownership, gathered)
+    )(jnp.transpose(vectors, (0, 2, 1, 3)), permeability, counts, ownership)
 
 
 def solution(mesh):

time: 65.5 us -> 50.2 us (0.77)
  Pallas kernels: 61.3 us -> 47.5 us
  local copies, waits for them, and re-layouts: 3.32 us -> 1.87 us
    pallas_call x1, Pallas kernels: 57.1 us -> 47.5 us  [per_device(): pl.pallas_call(functools.partial(assemble_kernel, n_grp, n_sub), out_shap...]
    pallas_call x1 -> x0, Pallas kernels: 4.16 us -> none  [per_device(): pl.pallas_call(functools.partial(place_kernel, n_sub), out_shape=jax.Shap...]
    unnamed x5 -> x1, local copies, waits for them, and re-layouts: 3.32 us -> 1.87 us
where the time goes in v2:
time: 50.2 us; the launch traced here: 50 us
  Pallas kernels  47.5 us (95%)
  local copies, waits for them, and re-layouts  1.87 us (4%)
  between operations  0.66 us (1%)
    pallas_call x1, Pallas kernels, per_device(): pl.pallas_call(functools.partial(assemble_kernel, n_grp, n_sub), out_shap...  47.5 us
    unnamed x1, local copies, waits for them, and re-layouts  1.87 us

profile of v2, /device:TPU:1, one launch (start us, length us, event | category | flops | bytes accessed | tf_op | source)
XLA Modules:
  0.0 50.0 jit_solution(7183939693668583891)
XLA Ops:
  0.7 47.5 %shard_map.46 = f32[1,32,16,144]{3,2,1,0:T(8,128)} custom-call(f32[16,20,16,128]{3,2,1,0:T(8,128)} %bitcast.1, f32[16,16,128]{2,1,0:T(8,128)} %perm.1, s32[1,1]{1,0:T(1,128)S(6)} %copy.6.counts, s32[1,32]{1,0:T(1,128)} %ownership.1), custom_call_target="tpu_custom_call" | custom-call | tf_op jit(solution)/shard_map/pallas_call | solution.py:348
  48.1 1.9 %copy.7 = f32[1,32,16,144]{3,2,1,0:T(8,128)} copy(f32[1,32,16,144]{3,2,1,0:T(8,128)} %shard_map.46) | data formatting | bytes 589824

commit v3 on v2

v3 whole, which is shorter than its diff:
```python
import functools

import jax
import jax.numpy as jnp
from jax import lax
from jax.experimental import pallas as pl
from jax.experimental.pallas import tpu as pltpu
from jax.sharding import PartitionSpec as P

MESH = pl.DeviceIdType.MESH
KV = 16
OV = 2
CX = 16
CZ = 16
NY = 128
EXT = CZ + 2 * OV
GROUP = 4
MSG = 24


def harmonic(first_perm, second_perm):
    return 2.0 * first_perm * second_perm / (first_perm + second_perm)


def split(values):
    high = values.astype(jnp.bfloat16)
    low = (values - high.astype(jnp.float32)).astype(jnp.bfloat16)
    return high, low


def stack_split(values):
    pairs = [split(value) for value in values]
    high = jnp.concatenate([pair[0] for pair in pairs], axis=1)
    low = jnp.concatenate([pair[1] for pair in pairs], axis=1)
    return jnp.concatenate([high, low], axis=0)


def gram(first, second):
    return lax.dot_general(
        first, second, (((1,), (1,)), ((), ())), preferred_element_type=jnp.float32
    )


def fold(product):
    return (product[:KV, :KV] + product[:KV, KV:]) + (product[KV:, :KV] + product[KV:, KV:])


def assemble_kernel(n_grp, n_sub, vec, perm, counts, ownership, out, z, zup, zdn, xl, xr, xd,
                    pown, pzl, pzu, pxl, pxr, pc, fx, fz, fy, dg, ends, ex, ez, ey, ed, rim,
                    raw, wp1, wp2, wl, wr, pool,
                    load_sem, send_sem, recv_sem, all_send, all_recv, pair_send, pair_recv, known):
    s = lax.axis_index("sub")
    g = lax.axis_index("grp")
    up, down = lax.rem(s + 1, n_sub), lax.rem(s + n_sub - 1, n_sub)
    chip, core = s // 2, lax.rem(s, 2)
    n_chip = n_sub // 2
    mate = chip * 2 + 1 - core
    right, left = lax.rem(g + 1, n_grp), lax.rem(g + n_grp - 1, n_grp)

    for a in range(KV):
        pltpu.make_async_copy(
            vec.at[a], z.at[:, pl.ds(1, CX), a, :], load_sem.at[0]
        ).start()
    pltpu.make_async_copy(perm, pown, load_sem.at[1]).start()

    barrier = pltpu.get_barrier_semaphore()
    for tg in (left, right):
        for ts in (s, up, down):
            pl.semaphore_signal(barrier, inc=1, device_id=(tg, ts), device_id_type=MESH)
    for ts in (up, down):
        pl.semaphore_signal(barrier, inc=1, device_id=(g, ts), device_id_type=MESH)

    zero_block = jnp.zeros((KV, NY), jnp.float32)
    for r in range(EXT):
        z[r, 0] = zero_block
        z[r, CX + 1] = zero_block

    at_low, at_high = s == 0, s == n_sub - 1
    at_left, at_right = g == 0, g == n_grp - 1
    lane = lax.broadcasted_iota(jnp.int32, (CZ, NY), 1)
    level = lax.broadcasted_iota(jnp.int32, (CZ, NY), 0)

    def along_y(cells, lanes):
        upward = harmonic(cells, pltpu.roll(cells, NY - 1, 1))
        coupling = jnp.where(lanes == NY - 1, 0.0, upward)
        both = jnp.where(lanes == NY - 1, cells, upward) + jnp.where(
            lanes == 0, cells, pltpu.roll(upward, 1, 1)
        )
        return coupling, both

    pltpu.make_async_copy(perm, pown, load_sem.at[1]).wait()
    fx[0] = jnp.zeros((CZ, NY), jnp.float32)
    fx[CX] = jnp.zeros((CZ, NY), jnp.float32)

    def inner_faces(x, carry):
        fx[x] = harmonic(pown[x - 1], pown[x])
        return carry

    lax.fori_loop(1, CX, inner_faces, 0, unroll=5)

    def inner_coefficients(x, carry):
        own = pown[x]
        upward = jnp.where(level == CZ - 1, 0.0, harmonic(own, pltpu.roll(own, CZ - 1, 0)))
        coupling, both = along_y(own, lane)
        fz[x] = upward
        fy[x] = coupling
        dg[x] = (fx[x] + fx[x + 1]) + (upward + pltpu.roll(upward, 1, 0)) + both
        return carry

    lax.fori_loop(0, CX, inner_coefficients, 0, unroll=8)

    whole = z.at[:, pl.ds(1, CX)]
    pltpu.make_async_copy(whole, whole, load_sem.at[0]).wait()
    count = counts[0, 0]
    own_rows = (lax.broadcasted_iota(jnp.int32, (KV, NY), 0) < count).astype(jnp.float32)
    low_keep = own_rows * (s > 0).astype(jnp.float32)
    high_keep = own_rows * (s < n_sub - 1).astype(jnp.float32)

    def keep_of(r):
        return low_keep if r < OV else high_keep if r >= EXT - OV else own_rows

    def mask_ends(x, carry):
        for r in (0, 1, 2, EXT - 2, EXT - 1):
            z[r, x] = z[r, x] * keep_of(r)
        return carry

    lax.fori_loop(1, CX + 1, mask_ends, 0, unroll=4)

    def mask_sides(r, carry):
        z[r, 1] = z[r, 1] * own_rows
        z[r, CX] = z[r, CX] * own_rows
        return carry

    lax.fori_loop(3, EXT - 2, mask_sides, 0, unroll=5)

    pl.semaphore_wait(barrier, 8)

    def tell(step):
        reach = 1 << step
        for ts in (lax.rem(s + reach, n_sub), lax.rem(s + n_sub - reach, n_sub)):
            pl.semaphore_signal(known.at[step], inc=1, device_id=(g, ts), device_id_type=MESH)

    def send(slot, src, dst, tg, ts):
        copy = pltpu.make_async_remote_copy(
            src_ref=src, dst_ref=dst, send_sem=send_sem.at[slot], recv_sem=recv_sem.at[slot],
            device_id=(tg, ts), device_id_type=MESH,
        )
        copy.start()
        return copy

    half = CZ // 2
    perm_copies = [
        send(0, perm.at[:, pl.ds(half, half), :], pzl, g, up),
        send(1, perm.at[:, pl.ds(0, half), :], pzu, g, down),
        send(2, perm.at[CX - 1], pxl, right, s),
        send(3, perm.at[0], pxr, left, s),
        send(4, perm.at[CX - 1, pl.ds(half, half), :], pc.at[0], right, up),
        send(5, perm.at[CX - 1, pl.ds(0, half), :], pc.at[1], right, down),
        send(6, perm.at[0, pl.ds(half, half), :], pc.at[2], left, up),
        send(7, perm.at[0, pl.ds(0, half), :], pc.at[3], left, down),
    ]
    vec_copies = [
        send(8, z.at[pl.ds(0, 3), pl.ds(1, CX)], zup, g, down),
        send(9, z.at[pl.ds(EXT - 2, 2), pl.ds(1, CX)], zdn, g, up),
        send(10, z.at[:, 1], xr, left, s),
        send(11, z.at[:, CX], xl, right, s),
        send(12, z.at[pl.ds(EXT - 4, 4), CX], xd.at[0], right, up),
        send(13, z.at[pl.ds(0, 4), CX], xd.at[1], right, down),
        send(14, z.at[pl.ds(EXT - 4, 4), 1], xd.at[2], left, up),
        send(15, z.at[pl.ds(0, 4), 1], xd.at[3], left, down),
    ]
    tell(0)

    def column(x, total):
        for first in range(0, CZ, GROUP):
            mine, applied = [], []
            for i in range(first, first + GROUP):
                r = i + OV
                here = z[r, x + 1]
                along = fy[x, i : i + 1, :]
                result = dg[x, i : i + 1, :] * here
                result = result - fx[x, i : i + 1, :] * z[r, x]
                result = result - fx[x + 1, i : i + 1, :] * z[r, x + 2]
                if i > 0:
                    result = result - fz[x, i - 1 : i, :] * z[r - 1, x + 1]
                if i < CZ - 1:
                    result = result - fz[x, i : i + 1, :] * z[r + 1, x + 1]
                result = result - along * pltpu.roll(here, NY - 1, 1)
                result = result - pltpu.roll(along * here, 1, 1)
                mine.append(here)
                applied.append(result)
                if i < 2:
                    raw[x, i] = result
                if i >= CZ - 2:
                    raw[x, i - CZ + 4] = result
            total = total + gram(stack_split(mine), stack_split(applied))
        return total

    total = jnp.zeros((2 * KV, 2 * KV), jnp.float32)
    total = lax.fori_loop(0, 4, column, total, unroll=2)
    pl.semaphore_wait(known.at[0], 2)
    tell(1)
    total = lax.fori_loop(4, 10, column, total, unroll=2)
    pl.semaphore_wait(known.at[1], 2)
    tell(2)
    total = lax.fori_loop(10, CX, column, total, unroll=2)

    for copy in perm_copies:
        copy.wait_recv()

    def gather_ends(x, carry):
        own = pown[x]
        first, last = own[0:1], own[CZ - 1 : CZ]
        low = jnp.where(at_low, jnp.broadcast_to(first, (3, NY)), pzl[x, half - 3 : half])
        high = jnp.where(at_high, jnp.broadcast_to(last, (3, NY)), pzu[x, 0:3])
        ends[x, 0:3] = low
        ends[x, 3:4] = first
        ends[x, 4:5] = last
        ends[x, 5:8] = high
        return carry

    lax.fori_loop(0, CX, gather_ends, 0, unroll=8)
    ex[0] = jnp.zeros((8, NY), jnp.float32)
    ex[CX] = jnp.zeros((8, NY), jnp.float32)

    def end_faces(x, carry):
        ex[x] = harmonic(ends[x - 1], ends[x])
        return carry

    lax.fori_loop(1, CX, end_faces, 0, unroll=15)

    def end_coefficients(x, carry):
        own = ends[x]
        upward = harmonic(own, pltpu.roll(own, 7, 0))
        coupling, both = along_y(own, lane[0:8])
        ez[x] = upward
        ey[x] = coupling
        ed[x] = (ex[x] + ex[x + 1]) + (upward + pltpu.roll(upward, 1, 0)) + both
        return carry

    lax.fori_loop(0, CX, end_coefficients, 0, unroll=16)
    for side, at_edge, own_x, face, low, high in (
        (0, at_left, 0, pxl, 0, 1), (1, at_right, CX - 1, pxr, 2, 3)
    ):
        rim[side, 2 : 2 + CZ] = harmonic(
            pown[own_x], jnp.where(at_edge, pown[own_x], face[...])
        )
        own = ends[own_x, 1:3]
        rim[side, 0:2] = harmonic(own, jnp.where(at_edge, own, pc[low, half - 2 : half]))
        own = ends[own_x, 5:7]
        rim[side, EXT - 2 : EXT] = harmonic(own, jnp.where(at_edge, own, pc[high, 0:2]))

    not_high = 1.0 - at_high.astype(jnp.float32)

    def end_column(x, total):
        mine = {r: z[r, x + 1] for r in (0, 1, 2, EXT - 3, EXT - 2, EXT - 1)}
        applied = {}
        for r, i in ((0, 1), (1, 2), (EXT - 2, 5), (EXT - 1, 6)):
            here = mine[r]
            along = ey[x, i : i + 1, :]
            result = ed[x, i : i + 1, :] * here
            result = result - ex[x, i : i + 1, :] * z[r, x]
            result = result - ex[x + 1, i : i + 1, :] * z[r, x + 2]
            if r > 0:
                result = result - ez[x, i - 1 : i, :] * mine[r - 1]
            if r < EXT - 1:
                result = result - ez[x, i : i + 1, :] * mine[r + 1]
            result = result - along * pltpu.roll(here, NY - 1, 1)
            applied[r] = result - pltpu.roll(along * here, 1, 1)
        low_face, high_face = ez[x, 2:3, :], ez[x, 4:5, :]
        applied[2] = low_face * (mine[2] - mine[1])
        kept = high_face * mine[EXT - 3]
        applied[EXT - 3] = kept - high_face * mine[EXT - 2]
        raw[x, 0] = raw[x, 0] + applied[2]
        raw[x, 3] = raw[x, 3] + kept
        raw[x, 4] = -(kept * not_high)
        order = sorted(mine)
        return total + gram(
            stack_split([mine[r] for r in order]), stack_split([applied[r] for r in order])
        )

    total = lax.fori_loop(0, CX, end_column, total, unroll=4)
    pl.semaphore_wait(known.at[2], 2)
    tell(3)

    for target, side, row in ((wl, 0, 1), (wr, 1, CX)):
        def side_weight(i, total, target=target, side=side, row=row):
            mine, weight = [], []
            for k in range(GROUP):
                here = z[i * GROUP + k, row]
                mine.append(here)
                weight.append(rim[side, pl.ds(i * GROUP + k, 1), :] * here)
            weight = stack_split(weight)
            target[i] = weight
            return total + gram(stack_split(mine), weight)

        total = lax.fori_loop(0, EXT // GROUP, side_weight, total, unroll=5)
        for i, r in ((0, 2), (1, 3), (2, EXT - 4), (3, EXT - 3)):
            raw[row - 1, i] = raw[row - 1, i] + rim[side, r : r + 1, :] * z[r, row]

    def finish_weights(x, carry):
        wp2[x] = stack_split([raw[x, 0], raw[x, 1]])
        wp1[x] = stack_split([raw[x, 2], raw[x, 3], raw[x, 4]])
        return carry

    lax.fori_loop(0, CX, finish_weights, 0, unroll=8)

    row_keep = lax.broadcasted_iota(jnp.int32, (KV, KV), 0) < count
    col_keep = lax.broadcasted_iota(jnp.int32, (KV, KV), 1) < count
    blocks = {4: jnp.where(row_keep & col_keep, fold(total), 0.0)}

    vec_copies[0].wait_recv()

    def upper_pair(x, carry):
        theirs = stack_split([zup[0, x], zup[1, x], zup[2, x]])
        return carry[0] + gram(wp1[x], theirs), carry[1] + gram(theirs, wp1[x])

    zeros = jnp.zeros((2 * KV, 2 * KV), jnp.float32)
    straight, turned = lax.fori_loop(0, CX, upper_pair, (zeros, zeros), unroll=16)
    blocks[5] = jnp.where(row_keep, fold(straight), 0.0)
    blocks[9] = jnp.where(col_keep, fold(turned), 0.0)

    vec_copies[1].wait_recv()

    def lower_pair(x, carry):
        theirs = stack_split([zdn[0, x], zdn[1, x]])
        return carry[0] + gram(wp2[x], theirs), carry[1] + gram(theirs, wp2[x])

    straight, turned = lax.fori_loop(0, CX, lower_pair, (zeros, zeros), unroll=16)
    blocks[3] = jnp.where(row_keep, fold(straight), 0.0)
    blocks[10] = jnp.where(col_keep, fold(turned), 0.0)

    for copy in vec_copies[2:]:
        copy.wait_recv()
    left_on = -(1.0 - at_left.astype(jnp.float32))
    right_on = -(1.0 - at_right.astype(jnp.float32))
    for base, on, weight, face, low, high in ((0, left_on, wl, xl, 0, 1), (6, right_on, wr, xr, 2, 3)):
        def side_pair(i, total, weight=weight, face=face):
            theirs = stack_split([face[i * GROUP + k] for k in range(GROUP)])
            return total + gram(weight[i], theirs)

        product = lax.fori_loop(0, EXT // GROUP, side_pair, zeros, unroll=5)
        blocks[base + 1] = jnp.where(row_keep, fold(product) * on, 0.0)
        theirs = stack_split([xd[low, r] for r in range(4)])
        blocks[base] = jnp.where(row_keep, fold(gram(weight[0], theirs)) * on, 0.0)
        theirs = stack_split([xd[high, r] for r in range(4)])
        blocks[base + 2] = jnp.where(
            row_keep, fold(gram(weight[EXT // GROUP - 1], theirs)) * on, 0.0
        )

    msg = pool.at[chip, core]
    msg[0:KV, :] = jnp.concatenate([blocks[i] for i in range(8)], axis=1)
    half_v = KV // 2
    gap = jnp.zeros((half_v, KV), jnp.float32)
    parts = [blocks[8][:half_v], blocks[8][half_v:], gap, blocks[9][:half_v], blocks[9][half_v:],
             blocks[10][:half_v], blocks[10][half_v:], gap]
    msg[KV:, :] = jnp.concatenate(parts, axis=1)

    pl.semaphore_wait(known.at[3], 2)

    def share(k, carry):
        pltpu.make_async_remote_copy(
            src_ref=msg, dst_ref=msg, send_sem=all_send, recv_sem=all_recv,
            device_id=(g, lax.rem(s + n_sub // 2 + 2 * k, n_sub)), device_id_type=MESH,
        ).start()
        return carry

    lax.fori_loop(0, n_chip // 2, share, 0)
    lax.fori_loop(n_chip // 2 + 1, n_chip, share, 0)
    for copy in perm_copies + vec_copies:
        copy.wait_send()
    rest = pool.at[pl.ds(0, n_chip - 1), 0]
    pltpu.make_async_copy(rest, rest, all_recv).wait()
    mine = pool.at[:, core]
    pair = pltpu.make_async_remote_copy(
        src_ref=mine, dst_ref=mine, send_sem=pair_send, recv_sem=pair_recv,
        device_id=(g, mate), device_id_type=MESH,
    )
    pair.start()
    pair.wait_recv()

    lane = lax.broadcasted_iota(jnp.int32, (half_v, NY), 1)
    from_below = (lane >= 3 * KV) & (lane < 4 * KV)
    from_above = (lane >= 5 * KV) & (lane < 6 * KV)

    def place(j, carry):
        row = ownership[0, j]
        before, after = jnp.maximum(row - 1, 0), jnp.minimum(row + 1, n_sub - 1)
        below = pool[before // 2, lax.rem(before, 2), KV:, :]
        above = pool[after // 2, lax.rem(after, 2), KV:, :]
        extra = pool[row // 2, lax.rem(row, 2), KV:, :]
        added = jnp.where(from_below & (row > 0), below, 0.0)
        added = added + jnp.where(from_above & (row < n_sub - 1), above, 0.0)
        top = pool[row // 2, lax.rem(row, 2), :half_v, :]
        bottom = pool[row // 2, lax.rem(row, 2), half_v:KV, :]
        shift = NY - KV
        below = pltpu.roll(below, shift, 1)
        above = pltpu.roll(above, shift, 1)
        out[0, j, :half_v, NY:] = extra[:, :KV]
        out[0, j, half_v:, NY:] = pltpu.roll(extra, shift, 1)[:, :KV]
        out[0, j, :half_v, 0:NY] = top + added
        added = jnp.where(from_below & (row > 0), below, 0.0)
        added = added + jnp.where(from_above & (row < n_sub - 1), above, 0.0)
        out[0, j, half_v:, 0:NY] = bottom + added
        return carry

    lax.fori_loop(0, n_sub, place, 0, unroll=8)
    pair.wait_send()
    pltpu.make_async_copy(rest, rest, all_send).wait()


def per_device(n_grp, n_sub, vectors, permeability, counts, ownership):
    f32, bf16 = jnp.float32, jnp.bfloat16
    vmem = pltpu.VMEM
    return pl.pallas_call(
        functools.partial(assemble_kernel, n_grp, n_sub),
        out_shape=jax.ShapeDtypeStruct((1, n_sub, KV, 9 * KV), f32),
        in_specs=[
            pl.BlockSpec(memory_space=pl.ANY),
            pl.BlockSpec(memory_space=pl.ANY),
            pl.BlockSpec(memory_space=pltpu.SMEM),
            pl.BlockSpec(memory_space=pltpu.SMEM),
        ],
        out_specs=pl.BlockSpec(memory_space=pltpu.VMEM),
        scratch_shapes=[
            vmem((EXT, CX + 2, KV, NY), f32),
            vmem((3, CX, KV, NY), f32),
            vmem((2, CX, KV, NY), f32),
            vmem((EXT, KV, NY), f32),
            vmem((EXT, KV, NY), f32),
            vmem((4, 4, KV, NY), f32),
            vmem((CX, CZ, NY), f32),
            vmem((CX, CZ // 2, NY), f32),
            vmem((CX, CZ // 2, NY), f32),
            vmem((CZ, NY), f32),
            vmem((CZ, NY), f32),
            vmem((4, CZ // 2, NY), f32),
            vmem((CX + 1, CZ, NY), f32),
            vmem((CX, CZ, NY), f32),
            vmem((CX, CZ, NY), f32),
            vmem((CX, CZ, NY), f32),
            vmem((CX, 8, NY), f32),
            vmem((CX + 1, 8, NY), f32),
            vmem((CX, 8, NY), f32),
            vmem((CX, 8, NY), f32),
            vmem((CX, 8, NY), f32),
            vmem((2, EXT, NY), f32),
            vmem((CX, 5, KV, NY), f32),
            vmem((CX, 2 * KV, 3 * NY), bf16),
            vmem((CX, 2 * KV, 2 * NY), bf16),
            vmem((EXT // GROUP, 2 * KV, GROUP * NY), bf16),
            vmem((EXT // GROUP, 2 * KV, GROUP * NY), bf16),
            vmem((n_sub // 2, 2, MSG, NY), f32),
            pltpu.SemaphoreType.DMA((2,)),
            pltpu.SemaphoreType.DMA((16,)),
            pltpu.SemaphoreType.DMA((16,)),
            pltpu.SemaphoreType.DMA,
            pltpu.SemaphoreType.DMA,
            pltpu.SemaphoreType.DMA,
            pltpu.SemaphoreType.DMA,
            pltpu.SemaphoreType.REGULAR((4,)),
        ],
        compiler_params=pltpu.CompilerParams(
            collective_id=0, has_side_effects=True, vmem_limit_bytes=58 << 20
        ),
    )(jnp.transpose(vectors, (0, 2, 1, 3)), permeability, counts, ownership)


def solution(mesh):
    in_specs = (P(None, "grp", "sub", None), P("grp", "sub", None), P("grp", "sub"), P("grp", None))
    out_specs = P("grp", None, None, None)
    return jax.shard_map(
        functools.partial(per_device, mesh.shape["grp"], mesh.shape["sub"]),
        mesh=mesh, in_specs=in_specs, out_specs=out_specs, check_vma=False,
    )
```

time: 50.2 us -> 43 us (0.86)
  Pallas kernels: 47.5 us -> 40.2 us
    pallas_call x1, Pallas kernels: 47.5 us -> 40.2 us  [per_device(): pl.pallas_call(functools.partial(assemble_kernel, n_grp, n_sub), out_shap...]
where the time goes in v3:
time: 43 us; the launch traced here: 42.7 us
  Pallas kernels  40.2 us (93%)
  local copies, waits for them, and re-layouts  1.87 us (4%)
  between operations  0.66 us (2%)
    pallas_call x1, Pallas kernels, per_device(): pl.pallas_call(functools.partial(assemble_kernel, n_grp, n_sub), out_shap...  40.2 us
    unnamed x1, local copies, waits for them, and re-layouts  1.87 us

profile of v3, /device:TPU:1, one launch (start us, length us, event | category | flops | bytes accessed | tf_op | source)
XLA Modules:
  0.0 42.7 jit_solution(13056960761678561749)
XLA Ops:
  0.7 40.2 %shard_map.46 = f32[1,32,16,144]{3,2,1,0:T(8,128)} custom-call(f32[16,20,16,128]{3,2,1,0:T(8,128)} %bitcast.1, f32[16,16,128]{2,1,0:T(8,128)} %perm.1, s32[1,1]{1,0:T(1,128)S(6)} %copy.6.counts, s32[1,32]{1,0:T(1,128)} %ownership.1), custom_call_target="tpu_custom_call" | custom-call | tf_op jit(solution)/shard_map/pallas_call | solution.py:415
  40.9 1.9 %copy.7 = f32[1,32,16,144]{3,2,1,0:T(8,128)} copy(f32[1,32,16,144]{3,2,1,0:T(8,128)} %shard_map.46) | data formatting | bytes 589824

commit v4 on v3

--- a/solution.py
+++ b/solution.py
@@ -64,13 +64,28 @@
     pltpu.make_async_copy(perm, pown, load_sem.at[1]).start()
 
     barrier = pltpu.get_barrier_semaphore()
-    for tg in (left, right):
-        for ts in (s, up, down):
-            pl.semaphore_signal(barrier, inc=1, device_id=(tg, ts), device_id_type=MESH)
-    for ts in (up, down):
-        pl.semaphore_signal(barrier, inc=1, device_id=(g, ts), device_id_type=MESH)
+    has_left, has_right = g > 0, g < n_grp - 1
+    for there, tg in ((has_left, left), (has_right, right)):
+        @pl.when(there)
+        def _(tg=tg):
+            for ts in (s, up, down):
+                pl.semaphore_signal(barrier, inc=1, device_id=(tg, ts), device_id_type=MESH)
+    for reach in (1, 2, 4):
+        for ts in (lax.rem(s + reach, n_sub), lax.rem(s + n_sub - reach, n_sub)):
+            pl.semaphore_signal(barrier, inc=1, device_id=(g, ts), device_id_type=MESH)
 
     zero_block = jnp.zeros((KV, NY), jnp.float32)
+    for missing, face, ring, near in (
+        (g == 0, pxl, xl, (0, 1)), (g == n_grp - 1, pxr, xr, (2, 3))
+    ):
+        @pl.when(missing)
+        def _(face=face, ring=ring, near=near):
+            face[...] = jnp.zeros(face.shape, jnp.float32)
+            ring[...] = jnp.zeros(ring.shape, jnp.float32)
+            for i in near:
+                pc[i] = jnp.zeros(pc.shape[1:], jnp.float32)
+                xd[i] = jnp.zeros(xd.shape[1:], jnp.float32)
+
     for r in range(EXT):
         z[r, 0] = zero_block
         z[r, CX + 1] = zero_block
@@ -133,19 +148,15 @@
 
     lax.fori_loop(3, EXT - 2, mask_sides, 0, unroll=5)
 
-    pl.semaphore_wait(barrier, 8)
-
-    def tell(step):
-        reach = 1 << step
-        for ts in (lax.rem(s + reach, n_sub), lax.rem(s + n_sub - reach, n_sub)):
-            pl.semaphore_signal(known.at[step], inc=1, device_id=(g, ts), device_id_type=MESH)
+    pl.semaphore_wait(
+        barrier, 6 + 3 * has_left.astype(jnp.int32) + 3 * has_right.astype(jnp.int32)
+    )
 
     def send(slot, src, dst, tg, ts):
         copy = pltpu.make_async_remote_copy(
             src_ref=src, dst_ref=dst, send_sem=send_sem.at[slot], recv_sem=recv_sem.at[slot],
             device_id=(tg, ts), device_id_type=MESH,
         )
-        copy.start()
         return copy
 
     half = CZ // 2
@@ -169,7 +180,37 @@
         send(14, z.at[pl.ds(EXT - 4, 4), 1], xd.at[2], left, up),
         send(15, z.at[pl.ds(0, 4), 1], xd.at[3], left, down),
     ]
-    tell(0)
+    copies = perm_copies + vec_copies
+    to_left, to_right = (3, 6, 7, 10, 14, 15), (2, 4, 5, 11, 12, 13)
+    along = [i for i in range(len(copies)) if i not in to_left + to_right]
+    for group in (range(8), range(8, 16)):
+        for slots, there in ((along, None), (to_left, has_left), (to_right, has_right)):
+            def start(slots=slots, group=group):
+                for i in slots:
+                    if i in group:
+                        copies[i].start()
+
+            start() if there is None else pl.when(there)(start)
+
+    def received(group):
+        for slots, there in ((along, None), (to_right, has_left), (to_left, has_right)):
+            def wait(slots=slots):
+                for i in slots:
+                    if i in group:
+                        copies[i].wait_recv()
+
+            wait() if there is None else pl.when(there)(wait)
+
+    def sent():
+        for slots, there in ((along, None), (to_left, has_left), (to_right, has_right)):
+            def wait(slots=slots):
+                for i in slots:
+                    copies[i].wait_send()
+
+            wait() if there is None else pl.when(there)(wait)
+
+    for ts in (lax.rem(s + 4, n_sub), lax.rem(s + n_sub - 4, n_sub)):
+        pl.semaphore_signal(known, inc=1, device_id=(g, ts), device_id_type=MESH)
 
     def column(x, total):
         for first in range(0, CZ, GROUP):
@@ -198,15 +239,9 @@
 
     total = jnp.zeros((2 * KV, 2 * KV), jnp.float32)
     total = lax.fori_loop(0, 4, column, total, unroll=2)
-    pl.semaphore_wait(known.at[0], 2)
-    tell(1)
-    total = lax.fori_loop(4, 10, column, total, unroll=2)
-    pl.semaphore_wait(known.at[1], 2)
-    tell(2)
-    total = lax.fori_loop(10, CX, column, total, unroll=2)
-
-    for copy in perm_copies:
-        copy.wait_recv()
+    total = lax.fori_loop(4, CX, column, total, unroll=2)
+
+    received(range(8))
 
     def gather_ends(x, carry):
         own = pown[x]
@@ -280,8 +315,6 @@
         )
 
     total = lax.fori_loop(0, CX, end_column, total, unroll=4)
-    pl.semaphore_wait(known.at[2], 2)
-    tell(3)
 
     for target, side, row in ((wl, 0, 1), (wr, 1, CX)):
         def side_weight(i, total, target=target, side=side, row=row):
@@ -309,7 +342,7 @@
     col_keep = lax.broadcasted_iota(jnp.int32, (KV, KV), 1) < count
     blocks = {4: jnp.where(row_keep & col_keep, fold(total), 0.0)}
 
-    vec_copies[0].wait_recv()
+    received((8,))
 
     def upper_pair(x, carry):
         theirs = stack_split([zup[0, x], zup[1, x], zup[2, x]])
@@ -320,7 +353,7 @@
     blocks[5] = jnp.where(row_keep, fold(straight), 0.0)
     blocks[9] = jnp.where(col_keep, fold(turned), 0.0)
 
-    vec_copies[1].wait_recv()
+    received((9,))
 
     def lower_pair(x, carry):
         theirs = stack_split([zdn[0, x], zdn[1, x]])
@@ -330,8 +363,7 @@
     blocks[3] = jnp.where(row_keep, fold(straight), 0.0)
     blocks[10] = jnp.where(col_keep, fold(turned), 0.0)
 
-    for copy in vec_copies[2:]:
-        copy.wait_recv()
+    received(range(10, 16))
     left_on = -(1.0 - at_left.astype(jnp.float32))
     right_on = -(1.0 - at_right.astype(jnp.float32))
     for base, on, weight, face, low, high in ((0, left_on, wl, xl, 0, 1), (6, right_on, wr, xr, 2, 3)):
@@ -356,28 +388,54 @@
              blocks[10][:half_v], blocks[10][half_v:], gap]
     msg[KV:, :] = jnp.concatenate(parts, axis=1)
 
-    pl.semaphore_wait(known.at[3], 2)
-
-    def share(k, carry):
+    pl.semaphore_wait(known, 2)
+
+    def pass_on(origin, hops):
+        slot = pool.at[lax.rem(chip + n_chip + origin, n_chip), core]
         pltpu.make_async_remote_copy(
-            src_ref=msg, dst_ref=msg, send_sem=all_send, recv_sem=all_recv,
-            device_id=(g, lax.rem(s + n_sub // 2 + 2 * k, n_sub)), device_id_type=MESH,
+            src_ref=slot, dst_ref=slot, send_sem=all_send,
+            recv_sem=all_recv.at[(origin - hops) % n_chip],
+            device_id=(g, lax.rem(s + n_sub + 2 * hops, n_sub)), device_id_type=MESH,
         ).start()
-        return carry
-
-    lax.fori_loop(0, n_chip // 2, share, 0)
-    lax.fori_loop(n_chip // 2 + 1, n_chip, share, 0)
-    for copy in perm_copies + vec_copies:
-        copy.wait_send()
-    rest = pool.at[pl.ds(0, n_chip - 1), 0]
-    pltpu.make_async_copy(rest, rest, all_recv).wait()
-    mine = pool.at[:, core]
-    pair = pltpu.make_async_remote_copy(
-        src_ref=mine, dst_ref=mine, send_sem=pair_send, recv_sem=pair_recv,
-        device_id=(g, mate), device_id_type=MESH,
-    )
-    pair.start()
-    pair.wait_recv()
+
+    def arrived(origin):
+        slot = pool.at[lax.rem(chip + n_chip + origin, n_chip), core]
+        pltpu.make_async_copy(slot, slot, all_recv.at[origin % n_chip]).wait()
+
+    def hand_over(origin):
+        slot = pool.at[lax.rem(chip + n_chip + origin, n_chip), core]
+        pltpu.make_async_remote_copy(
+            src_ref=slot, dst_ref=slot, send_sem=pair_send, recv_sem=pair_recv,
+            device_id=(g, mate), device_id_type=MESH,
+        ).start()
+
+    for hops in (4, -4, 2, -2, 1, -1):
+        pass_on(0, hops)
+    hand_over(0)
+    arrived(-4)
+    for hops in (3, 2, 1, -1):
+        pass_on(-4, hops)
+
+    @pl.when(core == 0)
+    def _():
+        pass_on(-4, 4)
+
+    arrived(4)
+    for hops in (-3, -2, -1, 1):
+        pass_on(4, hops)
+
+    @pl.when(core == 1)
+    def _():
+        pass_on(4, -4)
+
+    hand_over(-4)
+    hand_over(4)
+    for origin in (1, -1, 2, -2, 3, -3, 5, -5, 6, -6, 7, -7, 8):
+        arrived(origin)
+        hand_over(origin)
+    sent()
+    theirs = pool.at[:, 0]
+    pltpu.make_async_copy(theirs, theirs, pair_recv).wait()
 
     lane = lax.broadcasted_iota(jnp.int32, (half_v, NY), 1)
     from_below = (lane >= 3 * KV) & (lane < 4 * KV)
@@ -405,7 +463,8 @@
         return carry
 
     lax.fori_loop(0, n_sub, place, 0, unroll=8)
-    pair.wait_send()
+    rest = pool.at[pl.ds(0, n_chip - 1), 0]
+    pltpu.make_async_copy(theirs, theirs, pair_send).wait()
     pltpu.make_async_copy(rest, rest, all_send).wait()
 
 
@@ -455,10 +514,10 @@
             pltpu.SemaphoreType.DMA((16,)),
             pltpu.SemaphoreType.DMA((16,)),
             pltpu.SemaphoreType.DMA,
+            pltpu.SemaphoreType.DMA((n_sub // 2,)),
             pltpu.SemaphoreType.DMA,
             pltpu.SemaphoreType.DMA,
-            pltpu.SemaphoreType.DMA,
-            pltpu.SemaphoreType.REGULAR((4,)),
+            pltpu.SemaphoreType.REGULAR,
         ],
         compiler_params=pltpu.CompilerParams(
             collective_id=0, has_side_effects=True, vmem_limit_bytes=58 << 20

time: 43 us -> 39.4 us (0.916)
  the two profiles are of different devices: /device:TPU:1 before, /device:TPU:5 now
where the time goes in v4:
time: 39.4 us; the launch traced here: 39.1 us
  Pallas kernels  36.6 us (93%)
  local copies, waits for them, and re-layouts  1.87 us (5%)
  between operations  0.66 us (2%)
    pallas_call x1, Pallas kernels, per_device(): pl.pallas_call(functools.partial(assemble_kernel, n_grp, n_sub), out_shap...  36.6 us
    unnamed x1, local copies, waits for them, and re-layouts  1.87 us

profile of v4, /device:TPU:5, one launch (start us, length us, event | category | flops | bytes accessed | tf_op | source)
XLA Modules:
  0.0 39.1 jit_solution(5505585827605733934)
XLA Ops:
  0.7 36.6 %shard_map.46 = f32[1,32,16,144]{3,2,1,0:T(8,128)} custom-call(f32[16,20,16,128]{3,2,1,0:T(8,128)} %bitcast.1, f32[16,16,128]{2,1,0:T(8,128)} %perm.1, s32[1,1]{1,0:T(1,128)S(6)} %copy.6.counts, s32[1,32]{1,0:T(1,128)} %ownership.1), custom_call_target="tpu_custom_call" | custom-call | tf_op jit(solution)/shard_map/pallas_call | solution.py:474
  37.3 1.9 %copy.7 = f32[1,32,16,144]{3,2,1,0:T(8,128)} copy(f32[1,32,16,144]{3,2,1,0:T(8,128)} %shard_map.46) | data formatting | bytes 589824

commit v5 on v4

--- a/solution.py
+++ b/solution.py
@@ -124,30 +124,6 @@
 
     lax.fori_loop(0, CX, inner_coefficients, 0, unroll=8)
 
-    whole = z.at[:, pl.ds(1, CX)]
-    pltpu.make_async_copy(whole, whole, load_sem.at[0]).wait()
-    count = counts[0, 0]
-    own_rows = (lax.broadcasted_iota(jnp.int32, (KV, NY), 0) < count).astype(jnp.float32)
-    low_keep = own_rows * (s > 0).astype(jnp.float32)
-    high_keep = own_rows * (s < n_sub - 1).astype(jnp.float32)
-
-    def keep_of(r):
-        return low_keep if r < OV else high_keep if r >= EXT - OV else own_rows
-
-    def mask_ends(x, carry):
-        for r in (0, 1, 2, EXT - 2, EXT - 1):
-            z[r, x] = z[r, x] * keep_of(r)
-        return carry
-
-    lax.fori_loop(1, CX + 1, mask_ends, 0, unroll=4)
-
-    def mask_sides(r, carry):
-        z[r, 1] = z[r, 1] * own_rows
-        z[r, CX] = z[r, CX] * own_rows
-        return carry
-
-    lax.fori_loop(3, EXT - 2, mask_sides, 0, unroll=5)
-
     pl.semaphore_wait(
         barrier, 6 + 3 * has_left.astype(jnp.int32) + 3 * has_right.astype(jnp.int32)
     )
@@ -161,8 +137,8 @@
 
     half = CZ // 2
     perm_copies = [
-        send(0, perm.at[:, pl.ds(half, half), :], pzl, g, up),
-        send(1, perm.at[:, pl.ds(0, half), :], pzu, g, down),
+        send(0, perm.at[:, pl.ds(CZ - 3, 3), :], pzl, g, up),
+        send(1, perm.at[:, pl.ds(0, 3), :], pzu, g, down),
         send(2, perm.at[CX - 1], pxl, right, s),
         send(3, perm.at[0], pxr, left, s),
         send(4, perm.at[CX - 1, pl.ds(half, half), :], pc.at[0], right, up),
@@ -183,9 +159,9 @@
     copies = perm_copies + vec_copies
     to_left, to_right = (3, 6, 7, 10, 14, 15), (2, 4, 5, 11, 12, 13)
     along = [i for i in range(len(copies)) if i not in to_left + to_right]
-    for group in (range(8), range(8, 16)):
+    def start_all(group):
         for slots, there in ((along, None), (to_left, has_left), (to_right, has_right)):
-            def start(slots=slots, group=group):
+            def start(slots=slots):
                 for i in slots:
                     if i in group:
                         copies[i].start()
@@ -209,6 +185,32 @@
 
             wait() if there is None else pl.when(there)(wait)
 
+    start_all(range(8))
+    whole = z.at[:, pl.ds(1, CX)]
+    pltpu.make_async_copy(whole, whole, load_sem.at[0]).wait()
+    count = counts[0, 0]
+    own_rows = (lax.broadcasted_iota(jnp.int32, (KV, NY), 0) < count).astype(jnp.float32)
+    low_keep = own_rows * (s > 0).astype(jnp.float32)
+    high_keep = own_rows * (s < n_sub - 1).astype(jnp.float32)
+
+    def keep_of(r):
+        return low_keep if r < OV else high_keep if r >= EXT - OV else own_rows
+
+    def mask_ends(x, carry):
+        for r in (0, 1, 2, EXT - 2, EXT - 1):
+            z[r, x] = z[r, x] * keep_of(r)
+        return carry
+
+    lax.fori_loop(1, CX + 1, mask_ends, 0, unroll=4)
+
+    def mask_sides(r, carry):
+        z[r, 1] = z[r, 1] * own_rows
+        z[r, CX] = z[r, CX] * own_rows
+        return carry
+
+    lax.fori_loop(3, EXT - 2, mask_sides, 0, unroll=5)
+
+    start_all(range(8, 16))
     for ts in (lax.rem(s + 4, n_sub), lax.rem(s + n_sub - 4, n_sub)):
         pl.semaphore_signal(known, inc=1, device_id=(g, ts), device_id_type=MESH)
 
@@ -246,8 +248,8 @@
     def gather_ends(x, carry):
         own = pown[x]
         first, last = own[0:1], own[CZ - 1 : CZ]
-        low = jnp.where(at_low, jnp.broadcast_to(first, (3, NY)), pzl[x, half - 3 : half])
-        high = jnp.where(at_high, jnp.broadcast_to(last, (3, NY)), pzu[x, 0:3])
+        low = jnp.where(at_low, jnp.broadcast_to(first, (3, NY)), pzl[x])
+        high = jnp.where(at_high, jnp.broadcast_to(last, (3, NY)), pzu[x])
         ends[x, 0:3] = low
         ends[x, 3:4] = first
         ends[x, 4:5] = last
@@ -489,8 +491,8 @@
             vmem((EXT, KV, NY), f32),
             vmem((4, 4, KV, NY), f32),
             vmem((CX, CZ, NY), f32),
-            vmem((CX, CZ // 2, NY), f32),
-            vmem((CX, CZ // 2, NY), f32),
+            vmem((CX, 3, NY), f32),
+            vmem((CX, 3, NY), f32),
             vmem((CZ, NY), f32),
             vmem((CZ, NY), f32),
             vmem((4, CZ // 2, NY), f32),

time: 39.4 us -> 38.7 us (0.982)
  the two profiles are of different devices: /device:TPU:5 before, /device:TPU:7 now
where the time goes in v5:
time: 38.7 us; the launch traced here: 38.4 us
  Pallas kernels  35.9 us (93%)
  local copies, waits for them, and re-layouts  1.87 us (5%)
  between operations  0.66 us (2%)
    pallas_call x1, Pallas kernels, per_device(): pl.pallas_call(functools.partial(assemble_kernel, n_grp, n_sub), out_shap...  35.9 us
    unnamed x1, local copies, waits for them, and re-layouts  1.87 us

profile of v5, /device:TPU:7, one launch (start us, length us, event | category | flops | bytes accessed | tf_op | source)
XLA Modules:
  0.0 38.4 jit_solution(3630125065162125464)
XLA Ops:
  0.7 35.9 %shard_map.46 = f32[1,32,16,144]{3,2,1,0:T(8,128)} custom-call(f32[16,20,16,128]{3,2,1,0:T(8,128)} %bitcast.1, f32[16,16,128]{2,1,0:T(8,128)} %perm.1, s32[1,1]{1,0:T(1,128)S(6)} %copy.6.counts, s32[1,32]{1,0:T(1,128)} %ownership.1), custom_call_target="tpu_custom_call" | custom-call | tf_op jit(solution)/shard_map/pallas_call | solution.py:476
  36.6 1.9 %copy.7 = f32[1,32,16,144]{3,2,1,0:T(8,128)} copy(f32[1,32,16,144]{3,2,1,0:T(8,128)} %shard_map.46) | data formatting | bytes 589824

commit v6 on v5

--- a/solution.py
+++ b/solution.py
@@ -203,6 +203,8 @@
 
     lax.fori_loop(1, CX + 1, mask_ends, 0, unroll=4)
 
+    start_all((8, 9))
+
     def mask_sides(r, carry):
         z[r, 1] = z[r, 1] * own_rows
         z[r, CX] = z[r, CX] * own_rows
@@ -210,7 +212,7 @@
 
     lax.fori_loop(3, EXT - 2, mask_sides, 0, unroll=5)
 
-    start_all(range(8, 16))
+    start_all(range(10, 16))
     for ts in (lax.rem(s + 4, n_sub), lax.rem(s + n_sub - 4, n_sub)):
         pl.semaphore_signal(known, inc=1, device_id=(g, ts), device_id_type=MESH)
 
@@ -415,20 +417,22 @@
         pass_on(0, hops)
     hand_over(0)
     arrived(-4)
-    for hops in (3, 2, 1, -1):
-        pass_on(-4, hops)
 
     @pl.when(core == 0)
     def _():
         pass_on(-4, 4)
 
+    for hops in (3, 2, 1, -1):
+        pass_on(-4, hops)
+
     arrived(4)
-    for hops in (-3, -2, -1, 1):
-        pass_on(4, hops)
 
     @pl.when(core == 1)
     def _():
         pass_on(4, -4)
+
+    for hops in (-3, -2, -1, 1):
+        pass_on(4, hops)
 
     hand_over(-4)
     hand_over(4)

time: 38.7 us -> 37.7 us (0.974)
  the two profiles are of different devices: /device:TPU:7 before, /device:TPU:25 now
where the time goes in v6:
time: 37.7 us; the launch traced here: 37.5 us
  Pallas kernels  34.9 us (93%)
  local copies, waits for them, and re-layouts  1.87 us (5%)
  between operations  0.66 us (2%)
    pallas_call x1, Pallas kernels, per_device(): pl.pallas_call(functools.partial(assemble_kernel, n_grp, n_sub), out_shap...  34.9 us
    unnamed x1, local copies, waits for them, and re-layouts  1.87 us

profile of v6, /device:TPU:25, one launch (start us, length us, event | category | flops | bytes accessed | tf_op | source)
XLA Modules:
  0.0 37.5 jit_solution(4340250313815018436)
XLA Ops:
  0.7 34.9 %shard_map.46 = f32[1,32,16,144]{3,2,1,0:T(8,128)} custom-call(f32[16,20,16,128]{3,2,1,0:T(8,128)} %bitcast.1, f32[16,16,128]{2,1,0:T(8,128)} %perm.1, s32[1,1]{1,0:T(1,128)S(6)} %copy.6.counts, s32[1,32]{1,0:T(1,128)} %ownership.1), custom_call_target="tpu_custom_call" | custom-call | tf_op jit(solution)/shard_map/pallas_call | solution.py:480
  35.6 1.9 %copy.7 = f32[1,32,16,144]{3,2,1,0:T(8,128)} copy(f32[1,32,16,144]{3,2,1,0:T(8,128)} %shard_map.46) | data formatting | bytes 589824
